TPU v7x, 128 devices: a whole 4x4x4 slice. The times are simulated.
128 devices in a mesh: sx: 8 (over x_lo, z), sy: 16 (over y, x_hi, core).
Axes of the slice: x: 4 (x_hi: 2, x_lo: 2; x = x_hi * 2 + x_lo), y: 4, z: 4, core: 2. Of those that a mesh axis runs over, the one named last changes fastest.
Arguments:
- wave: bfloat16 [16, 128, 64, 512], P('sx', 'sy'), may hold values from -8 to 8
- potential: float32 [16, 128, 64], P('sx', 'sy'), may hold values from 0 to 2
- lower_cut: float32 [1], replicated, may hold values from 0.8 to 1.6
- upper_edge: float32 [1], replicated, may hold values from 5 to 6
Outputs:
- margin: float32 [512, 512], P('sy')
- projected: float32 [512, 512], P('sy')
All inputs are finite; a program needn't handle non-finite values.
Results may differ from a plain program's by a relative error of at most 0.0049.
Values may be sent and summed in bfloat16 or wider, within the bound.
A program may use at most 64 MiB of HBM per device.

v0:
```python
import jax
import jax.numpy as jnp
from jax import lax
from jax.sharding import PartitionSpec as P

STEPS = 4


def padded_2(array, sides, width):
    for axis, dim in sides:
        devices, length = (lax.axis_size(axis), array.shape[dim])
        up = [(i, (i + 1) % devices) for i in range(devices - 1)]
        down = [(j, i) for i, j in up]
        last = lax.slice_in_dim(array, length - width, length, axis=dim)
        leading = lax.slice_in_dim(array, 0, width, axis=dim)
        before = lax.ppermute(last, axis, up)
        after = lax.ppermute(leading, axis, down)
        array = jnp.concatenate([before, array, after], axis=dim)
    return array


def mass_line(field, axis):
    extent = field.shape[axis]
    below = lax.slice_in_dim(field, 0, extent - 2, axis=axis)
    middle = lax.slice_in_dim(field, 1, extent - 1, axis=axis)
    above = lax.slice_in_dim(field, 2, extent, axis=axis)
    return (4.0 * middle + below + above) / 6.0


def stiff_line(field, axis):
    extent = field.shape[axis]
    below = lax.slice_in_dim(field, 0, extent - 2, axis=axis)
    middle = lax.slice_in_dim(field, 1, extent - 1, axis=axis)
    above = lax.slice_in_dim(field, 2, extent, axis=axis)
    return 2.0 * middle - below - above


def operate(padded, potential):
    zpadded = jnp.pad(padded, ((0, 0), (0, 0), (1, 1), (0, 0)))
    mass_z = mass_line(zpadded, 2)
    stiff_z = stiff_line(zpadded, 2)
    first = stiff_line(mass_line(mass_z, 1), 0)
    second = mass_line(stiff_line(mass_z, 1), 0)
    third = mass_line(mass_line(stiff_z, 1), 0)
    centre_field = padded[1:-1, 1:-1]
    return 0.5 * (first + second + third) + potential[..., None] * centre_field


def extend(field):
    return padded_2(field, (("sx", 0), ("sy", 1)), 1)


def product(left, right):
    return lax.dot_general(
        left, right, (((0,), (0,)), ((), ())), preferred_element_type=jnp.float32
    )


def on_device(wave, potential, lower_cut, upper_edge):
    centre = 0.5 * (upper_edge[0] + lower_cut[0])
    radius = 0.5 * (upper_edge[0] - lower_cut[0])

    def apply_field(field):
        return operate(extend(field).astype(jnp.float32), potential)

    previous = wave
    current = ((apply_field(wave) - centre * wave.astype(jnp.float32)) / radius).astype(
        jnp.bfloat16
    )
    for _ in range(STEPS - 1):
        following = 2.0 * (apply_field(current) - centre * current.astype(jnp.float32)) / radius
        following = (following - previous.astype(jnp.float32)).astype(jnp.bfloat16)
        previous, current = (current, following)
    image = apply_field(current).astype(jnp.bfloat16)
    columns = wave.shape[3]
    nodes = (
        wave.shape[0] * lax.axis_size("sx") * wave.shape[1] * lax.axis_size("sy") * wave.shape[2]
    )
    flat_field = current.reshape(-1, columns)
    flat_image = image.reshape(-1, columns)
    margin_part = product(flat_field, flat_field) / nodes
    projected_part = product(flat_field, flat_image) / nodes
    margin_sum, projected_sum = lax.psum((margin_part, projected_part), ("sx", "sy"))
    share = columns // lax.axis_size("sy")
    offset = lax.axis_index("sy") * share
    margin = lax.dynamic_slice_in_dim(margin_sum, offset, share, 0)
    projected = lax.dynamic_slice_in_dim(projected_sum, offset, share, 0)
    return (margin, projected)


def solution(mesh):
    return jax.shard_map(
        on_device,
        mesh=mesh,
        in_specs=(P("sx", "sy", None, None), P("sx", "sy", None), P(), P()),
        out_specs=(P("sy", None), P("sy", None)),
        check_vma=False,
    )
```

profile of v0, /device:TPU:1, one launch (start us, length us, event | category | flops | bytes accessed | tf_op | source)
XLA Modules:
  0.0 360.3 jit_solution(14485406702156326867)
XLA Ops:
  8.5 4.4 %collective-permute-start = (bf16[1,8,64,512]{3,2,1,0:T(8,128)(2,1)S(1)}, bf16[1,8,64,512]{3,2,1,0:T(8,128)(2,1)S(1)}, u32[]{:S(2)}, u32[]{:S(2)}) collective-permute-start(bf16[1,8,64,512]{3,2,1,0:T(8,128)(2,1)S(1)} %get-tuple-element.43), channel_id=1, source_target_pairs={{0,16},{16,32},{32,48},{48,64},{64,80},{80,96},{96,112},{1,17},{17... | collective-permute-start | bytes 1572872 | tf_op jit(solution)/shard_map/ppermute | solution.py:16
  14.2 9.2 %collective-permute-done = bf16[1,8,64,512]{3,2,1,0:T(8,128)(2,1)S(1)} collective-permute-done((bf16[1,8,64,512]{3,2,1,0:T(8,128)(2,1)S(1)}, bf16[1,8,64,512]{3,2,1,0:T(8,128)(2,1)S(1)}, u32[]{:S(2)}, u32[]{:S(2)}) %collective-permute-start) | collective-permute-done | bytes 524320 | tf_op jit(solution)/shard_map/ppermute | solution.py:16
  23.5 1.3 constant_dynamic-update-slice_fusion.1
  24.8 2.8 collective-permute-done.1
  27.7 3.6 collective-permute-start.3
  31.3 4.5 %collective-permute-start.2 = (bf16[4,1,64,512]{3,2,1,0:T(8,128)(2,1)S(1)}, bf16[4,1,64,512]{3,2,1,0:T(8,128)(2,1)S(1)}, u32[]{:S(2)}, u32[]{:S(2)}) collective-permute-start(bf16[4,1,64,512]{3,2,1,0:T(8,128)(2,1)S(1)} %get-tuple-element.32), channel_id=1, source_target_pairs={{0,1},{1,2},{2,3},{3,4},{4,5},{5,6},{6,7},{7,8},{8,9},{9,10},{10,1... | collective-permute-start | bytes 786440 | tf_op jit(solution)/shard_map/ppermute | solution.py:16
  39.6 2.1 add_multiply_fusion.4
  42.4 1.8 add_multiply_fusion.9
  44.2 2.9 fusion.7
  48.5 4.0 %collective-permute-start.4 = (bf16[1,8,64,512]{3,2,1,0:T(8,128)(2,1)S(1)}, bf16[1,8,64,512]{3,2,1,0:T(8,128)(2,1)S(1)}, u32[]{:S(2)}, u32[]{:S(2)}) collective-permute-start(bf16[1,8,64,512]{3,2,1,0:T(8,128)(2,1)S(1)} %get-tuple-element.40), channel_id=1, source_target_pairs={{0,16},{16,32},{32,48},{48,64},{64,80},{80,96},{96,112},{1,17},{17... | collective-permute-start | bytes 1572872 | tf_op jit(solution)/shard_map/ppermute | solution.py:16
  52.5 6.6 %collective-permute-done.5 = bf16[1,8,64,512]{3,2,1,0:T(8,128)(2,1)S(1)} collective-permute-done((bf16[1,8,64,512]{3,2,1,0:T(8,128)(2,1)S(1)}, bf16[1,8,64,512]{3,2,1,0:T(8,128)(2,1)S(1)}, u32[]{:S(2)}, u32[]{:S(2)}) %collective-permute-start.5) | collective-permute-done | bytes 524320 | tf_op jit(solution)/shard_map/ppermute | solution.py:17
  59.1 1.8 collective-permute-done.4
  61.0 1.9 collective-permute-start.7
  62.9 8.1 %collective-permute-start.6 = (bf16[4,1,64,512]{3,2,1,0:T(8,128)(2,1)S(1)}, bf16[4,1,64,512]{3,2,1,0:T(8,128)(2,1)S(1)}, u32[]{:S(2)}, u32[]{:S(2)}) collective-permute-start(bf16[4,1,64,512]{3,2,1,0:T(8,128)(2,1)S(1)} %get-tuple-element.30), channel_id=1, source_target_pairs={{0,1},{1,2},{2,3},{3,4},{4,5},{5,6},{6,7},{7,8},{8,9},{9,10},{10,1... | collective-permute-start | bytes 786440 | tf_op jit(solution)/shard_map/ppermute | solution.py:16
  71.0 2.1 collective-permute-done.7
  74.9 2.1 add_multiply_fusion.3
  77.7 2.1 add_multiply_fusion.8
  79.8 3.0 fusion.8
  84.1 4.8 %collective-permute-start.8 = (bf16[1,8,64,512]{3,2,1,0:T(8,128)(2,1)S(1)}, bf16[1,8,64,512]{3,2,1,0:T(8,128)(2,1)S(1)}, u32[]{:S(2)}, u32[]{:S(2)}) collective-permute-start(bf16[1,8,64,512]{3,2,1,0:T(8,128)(2,1)S(1)} %get-tuple-element.38), channel_id=1, source_target_pairs={{0,16},{16,32},{32,48},{48,64},{64,80},{80,96},{96,112},{1,17},{17... | collective-permute-start | bytes 1572872 | tf_op jit(solution)/shard_map/ppermute | solution.py:16
  88.9 4.6 %collective-permute-done.9 = bf16[1,8,64,512]{3,2,1,0:T(8,128)(2,1)S(1)} collective-permute-done((bf16[1,8,64,512]{3,2,1,0:T(8,128)(2,1)S(1)}, bf16[1,8,64,512]{3,2,1,0:T(8,128)(2,1)S(1)}, u32[]{:S(2)}, u32[]{:S(2)}) %collective-permute-start.9) | collective-permute-done | bytes 524320 | tf_op jit(solution)/shard_map/ppermute | solution.py:17
  93.5 1.5 collective-permute-done.8
  95.0 1.9 collective-permute-start.11
  97.0 9.5 %collective-permute-start.10 = (bf16[4,1,64,512]{3,2,1,0:T(8,128)(2,1)S(1)}, bf16[4,1,64,512]{3,2,1,0:T(8,128)(2,1)S(1)}, u32[]{:S(2)}, u32[]{:S(2)}) collective-permute-start(bf16[4,1,64,512]{3,2,1,0:T(8,128)(2,1)S(1)} %get-tuple-element.28), channel_id=1, source_target_pairs={{0,1},{1,2},{2,3},{3,4},{4,5},{5,6},{6,7},{7,8},{8,9},{9,10},{10,1... | collective-permute-start | bytes 786440 | tf_op jit(solution)/shard_map/ppermute | solution.py:16
  106.5 1.9 collective-permute-done.11
  110.2 2.1 add_multiply_fusion.2
  113.0 2.1 add_multiply_fusion.7
  115.0 3.0 fusion.12
  118.1 1.3 collective-permute-start.13
  119.4 4.8 %collective-permute-start.12 = (bf16[1,8,64,512]{3,2,1,0:T(8,128)(2,1)S(1)}, bf16[1,8,64,512]{3,2,1,0:T(8,128)(2,1)S(1)}, u32[]{:S(2)}, u32[]{:S(2)}) collective-permute-start(bf16[1,8,64,512]{3,2,1,0:T(8,128)(2,1)S(1)} %get-tuple-element.36), channel_id=1, source_target_pairs={{0,16},{16,32},{32,48},{48,64},{64,80},{80,96},{96,112},{1,17},{17... | collective-permute-start | bytes 1572872 | tf_op jit(solution)/shard_map/ppermute | solution.py:16
  124.2 4.6 %collective-permute-done.13 = bf16[1,8,64,512]{3,2,1,0:T(8,128)(2,1)S(1)} collective-permute-done((bf16[1,8,64,512]{3,2,1,0:T(8,128)(2,1)S(1)}, bf16[1,8,64,512]{3,2,1,0:T(8,128)(2,1)S(1)}, u32[]{:S(2)}, u32[]{:S(2)}) %collective-permute-start.13) | collective-permute-done | bytes 524320 | tf_op jit(solution)/shard_map/ppermute | solution.py:17
  128.8 1.5 collective-permute-done.12
  130.3 1.9 collective-permute-start.15
  132.3 10.3 %collective-permute-start.14 = (bf16[4,1,64,512]{3,2,1,0:T(8,128)(2,1)S(1)}, bf16[4,1,64,512]{3,2,1,0:T(8,128)(2,1)S(1)}, u32[]{:S(2)}, u32[]{:S(2)}) collective-permute-start(bf16[4,1,64,512]{3,2,1,0:T(8,128)(2,1)S(1)} %get-tuple-element.26), channel_id=1, source_target_pairs={{0,1},{1,2},{2,3},{3,4},{4,5},{5,6},{6,7},{7,8},{8,9},{9,10},{10,1... | collective-permute-start | bytes 786440 | tf_op jit(solution)/shard_map/ppermute | solution.py:16
  142.5 2.1 collective-permute-done.15
  146.4 2.1 add_multiply_fusion.1
  149.2 2.1 add_multiply_fusion.6
  151.3 3.0 fusion.16
  155.7 5.3 %collective-permute-start.16 = (bf16[1,8,64,512]{3,2,1,0:T(8,128)(2,1)S(1)}, bf16[1,8,64,512]{3,2,1,0:T(8,128)(2,1)S(1)}, u32[]{:S(2)}, u32[]{:S(2)}) collective-permute-start(bf16[1,8,64,512]{3,2,1,0:T(8,128)(2,1)S(1)} %get-tuple-element.34), channel_id=1, source_target_pairs={{0,16},{16,32},{32,48},{48,64},{64,80},{80,96},{96,112},{1,17},{17... | collective-permute-start | bytes 1572872 | tf_op jit(solution)/shard_map/ppermute | solution.py:16
  161.0 4.6 %collective-permute-done.17 = bf16[1,8,64,512]{3,2,1,0:T(8,128)(2,1)S(1)} collective-permute-done((bf16[1,8,64,512]{3,2,1,0:T(8,128)(2,1)S(1)}, bf16[1,8,64,512]{3,2,1,0:T(8,128)(2,1)S(1)}, u32[]{:S(2)}, u32[]{:S(2)}) %collective-permute-start.17) | collective-permute-done | bytes 524320 | tf_op jit(solution)/shard_map/ppermute | solution.py:17
  165.6 1.5 collective-permute-done.16
  167.2 1.9 collective-permute-start.19
  169.1 9.7 %collective-permute-start.18 = (bf16[4,1,64,512]{3,2,1,0:T(8,128)(2,1)S(1)}, bf16[4,1,64,512]{3,2,1,0:T(8,128)(2,1)S(1)}, u32[]{:S(2)}, u32[]{:S(2)}) collective-permute-start(bf16[4,1,64,512]{3,2,1,0:T(8,128)(2,1)S(1)} %get-tuple-element.24), channel_id=1, source_target_pairs={{0,1},{1,2},{2,3},{3,4},{4,5},{5,6},{6,7},{7,8},{8,9},{9,10},{10,1... | collective-permute-start | bytes 786440 | tf_op jit(solution)/shard_map/ppermute | solution.py:16
  178.8 1.7 fusion.52
  182.4 2.1 add_multiply_fusion
  185.2 1.8 add_multiply_fusion.5
  187.0 3.1 fusion.51
  190.1 161.9 %all-reduce.8.cloned.1.call-done = (f32[512,512]{1,0:T(8,128)}, f32[512,512]{1,0:T(8,128)}) async-done(((f32[512,512]{1,0:T(8,128)}, f32[512,512]{1,0:T(8,128)}), (f32[512,512]{1,0:T(8,128)}, f32[512,512]{1,0:T(8,128)})) %all-reduce.8.cloned.1.call-update) | async-done | bytes 2097168 | tf_op jit(solution)/shard_map/psum | solution.py:83
  352.0 1.5 constant_dynamic-slice_fusion
  (45 shorter events, 20.4 us)
Async XLA Ops:
  7.2 344.8 %all-reduce.8.cloned.1.call-start = ((), (), s32[]{:S(2)}) async-start(), calls=%async_computation | async-start | bytes 4194304 | tf_op jit(solution)/shard_map/psum | solution.py:83
  8.5 15.0 %collective-permute-start = (bf16[1,8,64,512]{3,2,1,0:T(8,128)(2,1)S(1)}, bf16[1,8,64,512]{3,2,1,0:T(8,128)(2,1)S(1)}, u32[]{:S(2)}, u32[]{:S(2)}) collective-permute-start(bf16[1,8,64,512]{3,2,1,0:T(8,128)(2,1)S(1)} %get-tuple-element.43), channel_id=1, source_target_pairs={{0,16},{16,32},{32,48},{48,64},{64,80},{80,96},{96,112},{1,17},{17... | collective-permute-start | bytes 1572872 | tf_op jit(solution)/shard_map/ppermute | solution.py:16
  12.9 14.7 %collective-permute-start.1 = (bf16[1,8,64,512]{3,2,1,0:T(8,128)(2,1)S(1)}, bf16[1,8,64,512]{3,2,1,0:T(8,128)(2,1)S(1)}, u32[]{:S(2)}, u32[]{:S(2)}) collective-permute-start(bf16[1,8,64,512]{3,2,1,0:T(8,128)(2,1)S(1)} %get-tuple-element.42), channel_id=1, source_target_pairs={{16,0},{32,16},{48,32},{64,48},{80,64},{96,80},{112,96},{17,1},{33... | collective-permute-start | bytes 1572872 | tf_op jit(solution)/shard_map/ppermute | solution.py:17
  27.7 10.3 %collective-permute-start.3 = (bf16[4,1,64,512]{3,2,1,0:T(8,128)(2,1)S(1)}, bf16[4,1,64,512]{3,2,1,0:T(8,128)(2,1)S(1)}, u32[]{:S(2)}, u32[]{:S(2)}) collective-permute-start(bf16[4,1,64,512]{3,2,1,0:T(8,128)(2,1)S(1)} %get-tuple-element.33), channel_id=1, source_target_pairs={{1,0},{2,1},{3,2},{4,3},{5,4},{6,5},{7,6},{8,7},{9,8},{10,9},{11,1... | collective-permute-start | bytes 786440 | tf_op jit(solution)/shard_map/ppermute | solution.py:17
  31.3 7.9 %collective-permute-start.2 = (bf16[4,1,64,512]{3,2,1,0:T(8,128)(2,1)S(1)}, bf16[4,1,64,512]{3,2,1,0:T(8,128)(2,1)S(1)}, u32[]{:S(2)}, u32[]{:S(2)}) collective-permute-start(bf16[4,1,64,512]{3,2,1,0:T(8,128)(2,1)S(1)} %get-tuple-element.32), channel_id=1, source_target_pairs={{0,1},{1,2},{2,3},{3,4},{4,5},{5,6},{6,7},{7,8},{8,9},{9,10},{10,1... | collective-permute-start | bytes 786440 | tf_op jit(solution)/shard_map/ppermute | solution.py:16
  42.4 1.8 copy-start.2
  42.4 1.8 copy-start.4
  47.2 11.9 %collective-permute-start.5 = (bf16[1,8,64,512]{3,2,1,0:T(8,128)(2,1)S(1)}, bf16[1,8,64,512]{3,2,1,0:T(8,128)(2,1)S(1)}, u32[]{:S(2)}, u32[]{:S(2)}) collective-permute-start(bf16[1,8,64,512]{3,2,1,0:T(8,128)(2,1)S(1)} %get-tuple-element.41), channel_id=1, source_target_pairs={{16,0},{32,16},{48,32},{64,48},{80,64},{96,80},{112,96},{17,1},{33... | collective-permute-start | bytes 1572872 | tf_op jit(solution)/shard_map/ppermute | solution.py:17
  48.5 12.4 %collective-permute-start.4 = (bf16[1,8,64,512]{3,2,1,0:T(8,128)(2,1)S(1)}, bf16[1,8,64,512]{3,2,1,0:T(8,128)(2,1)S(1)}, u32[]{:S(2)}, u32[]{:S(2)}) collective-permute-start(bf16[1,8,64,512]{3,2,1,0:T(8,128)(2,1)S(1)} %get-tuple-element.40), channel_id=1, source_target_pairs={{0,16},{16,32},{32,48},{48,64},{64,80},{80,96},{96,112},{1,17},{17... | collective-permute-start | bytes 1572872 | tf_op jit(solution)/shard_map/ppermute | solution.py:16
  61.0 12.1 %collective-permute-start.7 = (bf16[4,1,64,512]{3,2,1,0:T(8,128)(2,1)S(1)}, bf16[4,1,64,512]{3,2,1,0:T(8,128)(2,1)S(1)}, u32[]{:S(2)}, u32[]{:S(2)}) collective-permute-start(bf16[4,1,64,512]{3,2,1,0:T(8,128)(2,1)S(1)} %get-tuple-element.31), channel_id=1, source_target_pairs={{1,0},{2,1},{3,2},{4,3},{5,4},{6,5},{7,6},{8,7},{9,8},{10,9},{11,1... | collective-permute-start | bytes 786440 | tf_op jit(solution)/shard_map/ppermute | solution.py:17
  62.9 11.4 %collective-permute-start.6 = (bf16[4,1,64,512]{3,2,1,0:T(8,128)(2,1)S(1)}, bf16[4,1,64,512]{3,2,1,0:T(8,128)(2,1)S(1)}, u32[]{:S(2)}, u32[]{:S(2)}) collective-permute-start(bf16[4,1,64,512]{3,2,1,0:T(8,128)(2,1)S(1)} %get-tuple-element.30), channel_id=1, source_target_pairs={{0,1},{1,2},{2,3},{3,4},{4,5},{5,6},{6,7},{7,8},{8,9},{9,10},{10,1... | collective-permute-start | bytes 786440 | tf_op jit(solution)/shard_map/ppermute | solution.py:16
  77.7 2.1 copy-start.3
  82.8 10.7 %collective-permute-start.9 = (bf16[1,8,64,512]{3,2,1,0:T(8,128)(2,1)S(1)}, bf16[1,8,64,512]{3,2,1,0:T(8,128)(2,1)S(1)}, u32[]{:S(2)}, u32[]{:S(2)}) collective-permute-start(bf16[1,8,64,512]{3,2,1,0:T(8,128)(2,1)S(1)} %get-tuple-element.39), channel_id=1, source_target_pairs={{16,0},{32,16},{48,32},{64,48},{80,64},{96,80},{112,96},{17,1},{33... | collective-permute-start | bytes 1572872 | tf_op jit(solution)/shard_map/ppermute | solution.py:17
  84.1 10.8 %collective-permute-start.8 = (bf16[1,8,64,512]{3,2,1,0:T(8,128)(2,1)S(1)}, bf16[1,8,64,512]{3,2,1,0:T(8,128)(2,1)S(1)}, u32[]{:S(2)}, u32[]{:S(2)}) collective-permute-start(bf16[1,8,64,512]{3,2,1,0:T(8,128)(2,1)S(1)} %get-tuple-element.38), channel_id=1, source_target_pairs={{0,16},{16,32},{32,48},{48,64},{64,80},{80,96},{96,112},{1,17},{17... | collective-permute-start | bytes 1572872 | tf_op jit(solution)/shard_map/ppermute | solution.py:16
  95.0 13.4 %collective-permute-start.11 = (bf16[4,1,64,512]{3,2,1,0:T(8,128)(2,1)S(1)}, bf16[4,1,64,512]{3,2,1,0:T(8,128)(2,1)S(1)}, u32[]{:S(2)}, u32[]{:S(2)}) collective-permute-start(bf16[4,1,64,512]{3,2,1,0:T(8,128)(2,1)S(1)} %get-tuple-element.29), channel_id=1, source_target_pairs={{1,0},{2,1},{3,2},{4,3},{5,4},{6,5},{7,6},{8,7},{9,8},{10,9},{11,1... | collective-permute-start | bytes 786440 | tf_op jit(solution)/shard_map/ppermute | solution.py:17
  97.0 12.6 %collective-permute-start.10 = (bf16[4,1,64,512]{3,2,1,0:T(8,128)(2,1)S(1)}, bf16[4,1,64,512]{3,2,1,0:T(8,128)(2,1)S(1)}, u32[]{:S(2)}, u32[]{:S(2)}) collective-permute-start(bf16[4,1,64,512]{3,2,1,0:T(8,128)(2,1)S(1)} %get-tuple-element.28), channel_id=1, source_target_pairs={{0,1},{1,2},{2,3},{3,4},{4,5},{5,6},{6,7},{7,8},{8,9},{9,10},{10,1... | collective-permute-start | bytes 786440 | tf_op jit(solution)/shard_map/ppermute | solution.py:16
  118.0 27.8 %copy-start = (bf16[2,8,64,512]{3,2,1,0:T(8,128)(2,1)}, bf16[2,8,64,512]{3,2,1,0:T(8,128)(2,1)S(1)}, u32[]{:S(2)}) copy-start(bf16[2,8,64,512]{3,2,1,0:T(8,128)(2,1)S(1)} %fusion.12) | copy-start | bytes 3145732
  118.1 10.7 %collective-permute-start.13 = (bf16[1,8,64,512]{3,2,1,0:T(8,128)(2,1)S(1)}, bf16[1,8,64,512]{3,2,1,0:T(8,128)(2,1)S(1)}, u32[]{:S(2)}, u32[]{:S(2)}) collective-permute-start(bf16[1,8,64,512]{3,2,1,0:T(8,128)(2,1)S(1)} %get-tuple-element.37), channel_id=1, source_target_pairs={{16,0},{32,16},{48,32},{64,48},{80,64},{96,80},{112,96},{17,1},{33... | collective-permute-start | bytes 1572872 | tf_op jit(solution)/shard_map/ppermute | solution.py:17
  119.4 10.8 %collective-permute-start.12 = (bf16[1,8,64,512]{3,2,1,0:T(8,128)(2,1)S(1)}, bf16[1,8,64,512]{3,2,1,0:T(8,128)(2,1)S(1)}, u32[]{:S(2)}, u32[]{:S(2)}) collective-permute-start(bf16[1,8,64,512]{3,2,1,0:T(8,128)(2,1)S(1)} %get-tuple-element.36), channel_id=1, source_target_pairs={{0,16},{16,32},{32,48},{48,64},{64,80},{80,96},{96,112},{1,17},{17... | collective-permute-start | bytes 1572872 | tf_op jit(solution)/shard_map/ppermute | solution.py:16
  130.3 14.3 %collective-permute-start.15 = (bf16[4,1,64,512]{3,2,1,0:T(8,128)(2,1)S(1)}, bf16[4,1,64,512]{3,2,1,0:T(8,128)(2,1)S(1)}, u32[]{:S(2)}, u32[]{:S(2)}) collective-permute-start(bf16[4,1,64,512]{3,2,1,0:T(8,128)(2,1)S(1)} %get-tuple-element.27), channel_id=1, source_target_pairs={{1,0},{2,1},{3,2},{4,3},{5,4},{6,5},{7,6},{8,7},{9,8},{10,9},{11,1... | collective-permute-start | bytes 786440 | tf_op jit(solution)/shard_map/ppermute | solution.py:17
  132.3 13.6 %collective-permute-start.14 = (bf16[4,1,64,512]{3,2,1,0:T(8,128)(2,1)S(1)}, bf16[4,1,64,512]{3,2,1,0:T(8,128)(2,1)S(1)}, u32[]{:S(2)}, u32[]{:S(2)}) collective-permute-start(bf16[4,1,64,512]{3,2,1,0:T(8,128)(2,1)S(1)} %get-tuple-element.26), channel_id=1, source_target_pairs={{0,1},{1,2},{2,3},{3,4},{4,5},{5,6},{6,7},{7,8},{8,9},{9,10},{10,1... | collective-permute-start | bytes 786440 | tf_op jit(solution)/shard_map/ppermute | solution.py:16
  149.2 2.1 copy-start.1
  154.4 11.2 %collective-permute-start.17 = (bf16[1,8,64,512]{3,2,1,0:T(8,128)(2,1)S(1)}, bf16[1,8,64,512]{3,2,1,0:T(8,128)(2,1)S(1)}, u32[]{:S(2)}, u32[]{:S(2)}) collective-permute-start(bf16[1,8,64,512]{3,2,1,0:T(8,128)(2,1)S(1)} %get-tuple-element.35), channel_id=1, source_target_pairs={{16,0},{32,16},{48,32},{64,48},{80,64},{96,80},{112,96},{17,1},{33... | collective-permute-start | bytes 1572872 | tf_op jit(solution)/shard_map/ppermute | solution.py:17
  155.7 11.4 %collective-permute-start.16 = (bf16[1,8,64,512]{3,2,1,0:T(8,128)(2,1)S(1)}, bf16[1,8,64,512]{3,2,1,0:T(8,128)(2,1)S(1)}, u32[]{:S(2)}, u32[]{:S(2)}) collective-permute-start(bf16[1,8,64,512]{3,2,1,0:T(8,128)(2,1)S(1)} %get-tuple-element.34), channel_id=1, source_target_pairs={{0,16},{16,32},{32,48},{48,64},{64,80},{80,96},{96,112},{1,17},{17... | collective-permute-start | bytes 1572872 | tf_op jit(solution)/shard_map/ppermute | solution.py:16
  167.2 13.5 %collective-permute-start.19 = (bf16[4,1,64,512]{3,2,1,0:T(8,128)(2,1)S(1)}, bf16[4,1,64,512]{3,2,1,0:T(8,128)(2,1)S(1)}, u32[]{:S(2)}, u32[]{:S(2)}) collective-permute-start(bf16[4,1,64,512]{3,2,1,0:T(8,128)(2,1)S(1)} %get-tuple-element.25), channel_id=1, source_target_pairs={{1,0},{2,1},{3,2},{4,3},{5,4},{6,5},{7,6},{8,7},{9,8},{10,9},{11,1... | collective-permute-start | bytes 786440 | tf_op jit(solution)/shard_map/ppermute | solution.py:17
  169.1 12.8 %collective-permute-start.18 = (bf16[4,1,64,512]{3,2,1,0:T(8,128)(2,1)S(1)}, bf16[4,1,64,512]{3,2,1,0:T(8,128)(2,1)S(1)}, u32[]{:S(2)}, u32[]{:S(2)}) collective-permute-start(bf16[4,1,64,512]{3,2,1,0:T(8,128)(2,1)S(1)} %get-tuple-element.24), channel_id=1, source_target_pairs={{0,1},{1,2},{2,3},{3,4},{4,5},{5,6},{6,7},{7,8},{8,9},{9,10},{10,1... | collective-permute-start | bytes 786440 | tf_op jit(solution)/shard_map/ppermute | solution.py:16
Sparse Core Ops, SparseCore 0:
  190.2 161.7 all-reduce.7
where the time goes:
time: 361 us; the launch traced here: 360 us
  waiting for transfers between devices  214 us (59%)
  starting transfers between devices  83.2 us (23%)
  other arithmetic  38.5 us (11%)
  between operations  15.8 us (4%)
  matrix products  4.76 us (1%)
  local copies, waits for them, and re-layouts  4.55 us (1%)
    psum x1, waiting for transfers between devices, on_device(): lax.psum((margin_part, projected_part), ('sx', 'sy'))  162 us
    ppermute x10, starting transfers between devices, padded_2(): before = lax.ppermute(last, axis, up)  65.4 us
    ppermute x10, waiting for transfers between devices, padded_2(): after = lax.ppermute(leading, axis, down)  30.3 us
    div x15, other arithmetic, mass_line(): return (4.0 * middle + below + above) / 6.0  23.6 us
    ppermute x10, waiting for transfers between devices, padded_2(): before = lax.ppermute(last, axis, up)  21.3 us
    ppermute x10, starting transfers between devices, padded_2(): after = lax.ppermute(leading, axis, down)  17.7 us
    convert_element_type x3, other arithmetic, on_device(): following = (following - previous.astype(jnp.float32)).astype(jnp.bfloat16)  8.96 us
  transfers between devices with their start and end apart: 21, of which 21 were waited for; matrix products, arithmetic and copies ran while one was open for 1% of the time, Pallas kernels for 0%

commit v1 on v0

v1 whole, which is shorter than its diff:
```python
import functools

import jax
import jax.numpy as jnp
import numpy as np
from jax import lax
from jax.experimental import pallas as pl
from jax.experimental.pallas import tpu as pltpu
from jax.sharding import PartitionSpec as P

MESH = pl.DeviceIdType.MESH
F32, BF16 = jnp.float32, jnp.bfloat16
GROUP = 32
NT = (((1,), (1,)), ((), ()))


def stencil_matrix():
    my, ky = np.zeros((4, 6)), np.zeros((4, 6))
    for i in range(4):
        my[i, i : i + 3] = 1, 4, 1
        ky[i, i : i + 3] = -1, 2, -1
    mz, kz = np.zeros((64, 64)), np.zeros((64, 64))
    for i in range(64):
        for j in range(max(i - 1, 0), min(i + 2, 64)):
            mz[i, j] = 4 if i == j else 1
            kz[i, j] = 2 if i == j else -1
    m = np.einsum("ij,kl->jlik", my, mz).reshape(6, 64, 256)
    g = np.einsum("ij,kl->jlik", ky, mz) + np.einsum("ij,kl->jlik", my, kz)
    g = g.reshape(6, 64, 256)
    p, q = 2 * m + 4 * g, g - m
    own = lambda t: t[1:5].reshape(256, 256)
    edge = lambda t: np.concatenate([t[5], t[0]], axis=0)
    return np.concatenate([own(p), own(q), own(q), edge(p), edge(q), edge(q)], axis=0)


def peer(k, z, x, c):
    dz, dx, dc = k % 4, (k // 4) % 4, k // 16
    sz = dz + c * (4 - 2 * dz)
    sx = dx + c * (4 - 2 * dx)
    return (z + sz) % 4, (x + sx) % 4, (c + dc) % 2


def source(k, z, x, c):
    dz, dx, dc = k % 4, (k // 4) % 4, k // 16
    cs = (c + dc) % 2
    sz = dz + cs * (4 - 2 * dz)
    sx = dx + cs * (4 - 2 * dx)
    return (z + 4 - sz % 4) % 4, (x + 4 - sx % 4) % 4, cs


def kernel(
    wave, pot, low, high, w_in, margin, projected,
    t, u0, u1, u2, u3, u4, img, d0, rf, ri, gm, part, other, half, rs, ob,
    in_s, in_r, pin_s, pin_r, hal_s, hal_r, phal_s, phal_r, edge_s, edge_r,
    f_s, f_r, i_s, i_r, core_s, core_r, rs_s, rs_r, ag_s, ag_r,
):
    sx, sy = lax.axis_index("sx"), lax.axis_index("sy")
    z, x = sx % 4, 2 * ((sy // 2) % 2) + sx // 4
    yy, c = sy // 4, sy % 2
    s4 = sy % 4
    j = sx * 4 + s4

    def mesh_id(zz, xx, cc, y):
        return ((xx % 2) * 4 + zz, y * 4 + (xx // 2) * 2 + cc)

    def index(zz, xx, cc):
        return ((xx % 2) * 4 + zz) * 4 + (xx // 2) * 2 + cc

    def remote(src, dst, ss, rr, dev):
        return pltpu.make_async_remote_copy(
            src_ref=src, dst_ref=dst, send_sem=ss, recv_sem=rr, device_id=dev, device_id_type=MESH
        )

    for u in (u0, u1, u2, u3, u4):
        u[0] = jnp.zeros(u.shape[1:], BF16)
        u[17] = jnp.zeros(u.shape[1:], BF16)
        for b in (0, 1, 10, 11):
            u[:, b] = jnp.zeros((18, 16, 256), BF16)
    d0[:, 0] = jnp.zeros((16, 1, 256), F32)
    d0[:, 9] = jnp.zeros((16, 1, 256), F32)

    barrier = pltpu.get_barrier_semaphore()

    @pl.loop(1, GROUP)
    def _(k):
        pl.semaphore_signal(
            barrier, inc=1, device_id=mesh_id(*peer(k, z, x, c), yy), device_id_type=MESH
        )

    for dy in (1, 2, 3):
        pl.semaphore_signal(
            barrier, inc=1, device_id=mesh_id(z, x, c, (yy + dy) % 4), device_id_type=MESH
        )

    eye = (
        lax.broadcasted_iota(jnp.int32, (256, 256), 0)
        == lax.broadcasted_iota(jnp.int32, (256, 256), 1)
    ).astype(F32).astype(BF16)
    for a in range(2):
        for b in range(2):
            nodes = wave[a, 4 * b : 4 * b + 4].reshape(256, 512)
            for h in range(2):
                t[a, b, 256 * h : 256 * h + 256] = lax.dot_general(
                    eye, nodes[:, 256 * h : 256 * h + 256], NT, preferred_element_type=F32
                ).astype(BF16)
            d0[2 * sx + a, 1 + 2 * s4 + b] = jnp.concatenate(
                [pot[a, 4 * b + i : 4 * b + i + 1, :] for i in range(4)], axis=1
            )

    pl.semaphore_wait(barrier, GROUP - 1 + 3)

    xs = pl.ds(1 + 2 * sx, 2)
    bs = pl.ds(2 + 2 * s4, 2)
    own_pot = d0.at[pl.ds(2 * sx, 2), pl.ds(1 + 2 * s4, 2)]

    def cols(i):
        return pl.ds(pl.multiple_of(16 * i, 16), 16)

    def in_copies(k):
        pz, px, pc = peer(k, z, x, c)
        dev = mesh_id(pz, px, pc, yy)
        rows = cols(index(pz, px, pc))
        return (
            remote(t.at[:, :, rows], u0.at[xs, bs], in_s.at[k], in_r.at[k], dev),
            remote(own_pot, own_pot, pin_s.at[k], pin_r.at[k], dev),
        )

    @pl.loop(1, GROUP)
    def _(k):
        for copy in in_copies(k):
            copy.start()

    u0[xs, bs] = t[:, :, cols(j)]

    def edge_copies(side, s):
        far = (yy + 3 + 2 * side) % 4
        mine, theirs = (2, 10) if side == 0 else (9, 1)
        dev = mesh_id(z, x, c, far)
        px = pl.ds(2 * s, 2)
        ux = pl.ds(1 + 2 * s, 2)
        return (
            remote(u0.at[ux, mine], u0.at[ux, theirs], hal_s.at[side, s], hal_r.at[side, s], dev),
            remote(
                d0.at[px, mine - 1], d0.at[px, theirs - 1],
                phal_s.at[side, s], phal_r.at[side, s], dev,
            ),
        )

    def send_on(s, quarter):
        @pl.when(jnp.logical_and(quarter == 0, yy > 0))
        def _():
            for copy in edge_copies(0, s):
                copy.start()

        @pl.when(jnp.logical_and(quarter == 3, yy < 3))
        def _():
            for copy in edge_copies(1, s):
                copy.start()

    send_on(sx, s4)

    @pl.loop(1, GROUP)
    def _(k):
        for copy in in_copies(k):
            copy.wait_recv()
        pz, px, pc = source(k, z, x, c)
        send_on((px % 2) * 4 + pz, (px // 2) * 2 + pc)

    centre = 0.5 * (high[0] + low[0])
    inv_radius = 1.0 / (0.5 * (high[0] - low[0]))

    def stencil(u, x0, lo, hi):
        n = hi - lo
        rows = 4 * n * 16
        own, edge = [], []
        for dx in (1, 0, 2):
            px = pl.ds(x0 + dx, 4)
            own.append(u[px, lo:hi].reshape(rows, 256))
            nxt = u[px, lo + 1 : hi + 1, :, 0:128].reshape(rows, 128)
            prv = u[px, lo - 1 : hi - 1, :, 128:256].reshape(rows, 128)
            first = lax.broadcasted_iota(jnp.int32, (rows, 128), 1) < 64
            edge.append(jnp.where(first, nxt, prv))
        lhs = jnp.concatenate(own + edge, axis=1)
        acc = jnp.dot(lhs, w_in[...], preferred_element_type=F32)
        return acc.reshape(4, n, 16, 256)

    def apply_step(u, prev, out, lo, hi):
        @pl.loop(0, 4)
        def _(i):
            x0 = 4 * i
            acc = stencil(u, x0, lo, hi)
            px = pl.ds(x0 + 1, 4)
            v = u[px, lo:hi].astype(F32)
            d = (d0[pl.ds(x0, 4), lo - 1 : hi - 1] - centre) * inv_radius
            if prev is None:
                res = acc * (inv_radius / 72.0) + d * v
            else:
                res = acc * (inv_radius / 36.0) + (2.0 * d) * v - prev[px, lo:hi].astype(F32)
            out[px, lo:hi] = res.astype(BF16)

    def outside_zero(out):
        @pl.when(yy == 0)
        def _():
            out[:, 1] = jnp.zeros((18, 16, 256), BF16)

        @pl.when(yy == 3)
        def _():
            out[:, 10] = jnp.zeros((18, 16, 256), BF16)

    apply_step(u0, None, u1, 3, 9)

    def halo_wait(side):
        for s in range(8):
            for copy in edge_copies(side, s):
                copy.wait_recv()

    @pl.when(yy < 3)
    def _():
        halo_wait(0)

    @pl.when(yy > 0)
    def _():
        halo_wait(1)

    apply_step(u0, None, u1, 1, 3)
    apply_step(u0, None, u1, 9, 11)
    outside_zero(u1)
    apply_step(u1, u0, u2, 1, 11)
    outside_zero(u2)
    apply_step(u2, u1, u3, 1, 11)
    outside_zero(u3)
    apply_step(u3, u2, u4, 2, 10)

    def layer(side):
        far = (yy + 3 + 2 * side) % 4
        mine, theirs, lanes = (2, 10, pl.ds(0, 128)) if side == 0 else (9, 1, pl.ds(128, 128))
        return remote(
            u4.at[pl.ds(1, 16), mine, :, lanes],
            u4.at[pl.ds(1, 16), theirs, :, lanes],
            edge_s.at[side], edge_r.at[side], mesh_id(z, x, c, far),
        )

    @pl.when(yy > 0)
    def _():
        layer(0).start()

    @pl.when(yy < 3)
    def _():
        layer(1).start()

    def out_copy(k, src, dst, ss, rr, first):
        pz, px, pc = peer(k, z, x, c)
        i = index(pz, px, pc)
        return remote(
            src.at[pl.ds(first + 2 * (i // 4), 2), pl.ds(2 * first + 2 * (i % 4), 2)],
            dst.at[:, :, cols(j)], ss.at[k], rr.at[k], mesh_id(pz, px, pc, yy),
        )

    @pl.loop(1, GROUP)
    def _(k):
        out_copy(k, u4, rf, f_s, f_r, 1).start()

    rf[:, :, cols(j)] = u4[xs, bs]

    @pl.when(yy < 3)
    def _():
        layer(0).wait_recv()

    @pl.when(yy > 0)
    def _():
        layer(1).wait_recv()

    @pl.loop(0, 4)
    def _(i):
        x0 = 4 * i
        acc = stencil(u4, x0, 2, 10)
        v = u4[pl.ds(x0 + 1, 4), 2:10].astype(F32)
        res = acc * (1.0 / 72.0) + d0[pl.ds(x0, 4), 1:9] * v
        img[pl.ds(x0, 4)] = res.astype(BF16)

    @pl.loop(1, GROUP)
    def _(k):
        out_copy(k, img, ri, i_s, i_r, 0).start()

    ri[:, :, cols(j)] = img[pl.ds(2 * sx, 2), pl.ds(2 * s4, 2)]

    def core_copy(n):
        return remote(
            part.at[n, :, 1 - c], other.at[n], core_s.at[n], core_r.at[n], (sx, sy + 1 - 2 * c)
        )

    def gram(n, right):
        whole = jnp.concatenate([rf[a, b] for a in range(2) for b in range(2)], axis=1)
        with_ = jnp.concatenate([right[a, b] for a in range(2) for b in range(2)], axis=1)
        for r in range(4):
            g = lax.dot_general(
                whole[128 * r : 128 * r + 128], with_, NT, preferred_element_type=F32
            ).reshape(2, 2, 2, 16, 512)
            gm[2 * r : 2 * r + 2] = g
            part[n, 2 * r : 2 * r + 2] = g.astype(BF16)
        core_copy(n).start()

    def rs_peer(k):
        dz, dx, dy = k % 4, (k // 4) % 4, k // 16
        tz = (z + dz + c * (4 - 2 * dz)) % 4
        tx = (x + dx + c * (4 - 2 * dx)) % 4
        ty = (yy + dy + c * (4 - 2 * dy)) % 4
        return mesh_id(tz, tx, c, ty)

    def rs_copy(n, k):
        dx, dy = rs_peer(k)
        return remote(
            half.at[n, dy // 2, dx // 4, :, pl.ds(pl.multiple_of(128 * (dx % 4), 128), 128)],
            rs.at[n, k], rs_s.at[n, k], rs_r.at[n, k], (dx, dy),
        )

    def scatter(n):
        core_copy(n).wait_recv()
        half[n] = (gm[:, c] + other[n].astype(F32)).astype(BF16)

        @pl.loop(1, 64)
        def _(k):
            rs_copy(n, k).start()

        rs[n, 0] = half[n, sy // 2, sx // 4, :, pl.ds(pl.multiple_of(128 * (sx % 4), 128), 128)]

    def collect(n):
        @pl.loop(1, 64)
        def _(k):
            rs_copy(n, k).wait_recv()

        ob[sx, n] = jnp.sum(rs[n].astype(F32), axis=0) * (1.0 / 131072.0)

    @pl.loop(1, GROUP)
    def _(k):
        out_copy(k, u4, rf, f_s, f_r, 1).wait_recv()

    gram(0, rf)
    scatter(0)

    @pl.loop(1, GROUP)
    def _(k):
        out_copy(k, img, ri, i_s, i_r, 0).wait_recv()

    gram(1, ri)
    scatter(1)
    collect(0)
    collect(1)

    def ag_copy(k):
        return remote(ob.at[sx], ob.at[sx], ag_s.at[k], ag_r.at[k], ((sx + k) % 8, sy))

    for k in range(1, 8):
        ag_copy(k).start()

    @pl.loop(1, GROUP)
    def _(k):
        for copy in in_copies(k):
            copy.wait_send()
        out_copy(k, u4, rf, f_s, f_r, 1).wait_send()
        out_copy(k, img, ri, i_s, i_r, 0).wait_send()

    def sent(s, quarter):
        @pl.when(jnp.logical_and(quarter == 0, yy > 0))
        def _():
            for copy in edge_copies(0, s):
                copy.wait_send()

        @pl.when(jnp.logical_and(quarter == 3, yy < 3))
        def _():
            for copy in edge_copies(1, s):
                copy.wait_send()

    @pl.loop(0, 8)
    def _(s):
        sent(s, 0)
        sent(s, 3)

    @pl.when(yy > 0)
    def _():
        layer(0).wait_send()

    @pl.when(yy < 3)
    def _():
        layer(1).wait_send()

    for n in range(2):
        core_copy(n).wait_send()

        @pl.loop(1, 64)
        def _(k):
            rs_copy(n, k).wait_send()

    for k in range(1, 8):
        ag_copy(k).wait()
    for s in range(8):
        rows, lanes = pl.ds(16 * (s // 4), 16), pl.ds(128 * (s % 4), 128)
        margin[rows, lanes] = ob[s, 0]
        projected[rows, lanes] = ob[s, 1]


def on_device(wave, potential, lower_cut, upper_edge):
    dma = pltpu.SemaphoreType.DMA
    field = pltpu.VMEM((18, 12, 16, 256), BF16)
    block = pltpu.VMEM((2, 2, 512, 256), BF16)
    vmem = pl.BlockSpec(memory_space=pltpu.VMEM)
    smem = pl.BlockSpec(memory_space=pltpu.SMEM)
    weights = jnp.asarray(stencil_matrix(), BF16)
    return pl.pallas_call(
        kernel,
        out_shape=[jax.ShapeDtypeStruct((32, 512), F32)] * 2,
        in_specs=[vmem, vmem, smem, smem, vmem],
        out_specs=[vmem, vmem],
        scratch_shapes=[
            block,
            field, field, field, field, field,
            pltpu.VMEM((16, 8, 16, 256), BF16),
            pltpu.VMEM((16, 10, 1, 256), F32),
            block, block,
            pltpu.VMEM((8, 2, 2, 16, 512), F32),
            pltpu.VMEM((2, 8, 2, 2, 16, 512), BF16),
            pltpu.VMEM((2, 8, 2, 16, 512), BF16),
            pltpu.VMEM((2, 8, 2, 16, 512), BF16),
            pltpu.VMEM((2, 64, 16, 128), BF16),
            pltpu.VMEM((8, 2, 16, 128), F32),
            dma((32,)), dma((32,)), dma((32,)), dma((32,)),
            dma((2, 8)), dma((2, 8)), dma((2, 8)), dma((2, 8)),
            dma((2,)), dma((2,)),
            dma((32,)), dma((32,)), dma((32,)), dma((32,)),
            dma((2,)), dma((2,)),
            dma((2, 64)), dma((2, 64)),
            dma((8,)), dma((8,)),
        ],
        compiler_params=pltpu.CompilerParams(
            collective_id=0, has_side_effects=True, vmem_limit_bytes=48 << 20
        ),
    )(wave, potential, lower_cut, upper_edge, weights)


def solution(mesh):
    return jax.shard_map(
        on_device,
        mesh=mesh,
        in_specs=(P("sx", "sy", None, None), P("sx", "sy", None), P(), P()),
        out_specs=(P("sy", None), P("sy", None)),
        check_vma=False,
    )
```

time: 361 us -> 91.4 us (0.25)
  waiting for transfers between devices: 214 us -> 0 us
  Pallas kernels: 0 us -> 85 us
  starting transfers between devices: 83.2 us -> 0 us
  other arithmetic: 38.5 us -> 0 us
  between operations: 15.8 us -> 1.94 us
  matrix products: 4.76 us -> 0 us
    psum x1 -> x0, waiting for transfers between devices: 162 us -> none  [on_device(): lax.psum((margin_part, projected_part), ('sx', 'sy'))]
    pallas_call x0 -> x1, Pallas kernels: none -> 85 us  [on_device(): pl.pallas_call(kernel, out_shape=[jax.ShapeDtypeStruct((32, 512), F32)] *...]
    ppermute x20 -> x0, starting transfers between devices: 83.1 us -> none  [the longest x10 65.4 us: padded_2(): before = lax.ppermute(last, axis, up)]
    ppermute x20 -> x0, waiting for transfers between devices: 51.7 us -> none  [the longest x10 30.3 us: padded_2(): after = lax.ppermute(leading, axis, down)]
    div x15 -> x0, other arithmetic: 23.6 us -> none  [mass_line(): return (4.0 * middle + below + above) / 6.0]
    convert_element_type x9 -> x0, other arithmetic: 14.6 us -> none  [the longest x3 8.96 us: on_device(): following = (following - previous.astype(jnp.float32)).astype(jnp.bfloat16)]
    dot_general x2 -> x0, matrix products: 4.76 us -> none  [product(): lax.dot_general(left, right, (((0,), (0,)), ((), ())), preferred_element_...]
  transfers between devices with their start and end apart: 21 -> 0, of which waited for: 21 -> 0; matrix products, arithmetic and copies ran while one was open for 1% -> 0% of each run, Pallas kernels for 0% -> 0%
where the time goes in v1:
time: 91.4 us; the launch traced here: 91.1 us
  Pallas kernels  85 us (93%)
  local copies, waits for them, and re-layouts  4.24 us (5%)
  between operations  1.94 us (2%)
    pallas_call x1, Pallas kernels, on_device(): pl.pallas_call(kernel, out_shape=[jax.ShapeDtypeStruct((32, 512), F32)] *...  85 us
    unnamed x8, local copies, waits for them, and re-layouts  4.24 us

profile of v1, /device:TPU:1, one launch (start us, length us, event | category | flops | bytes accessed | tf_op | source)
XLA Modules:
  0.0 91.1 jit_solution(9102612301880723858)
XLA Ops:
  1.9 0.0 copy-start
  1.9 1.2 %copy-done = bf16[2,8,64,512]{3,2,1,0:T(8,128)(2,1)S(1)} copy-done((bf16[2,8,64,512]{3,2,1,0:T(8,128)(2,1)S(1)}, bf16[2,8,64,512]{3,2,1,0:T(8,128)(2,1)}, u32[]{:S(2)}) %copy-start) | copy-done | bytes 1048600
  3.1 0.0 copy-start.1
  3.1 1.1 %copy-done.1 = bf16[1152,256]{1,0:T(8,128)(2,1)S(1)} copy-done((bf16[1152,256]{1,0:T(8,128)(2,1)S(1)}, bf16[1152,256]{1,0:T(8,128)(2,1)}, u32[]{:S(2)}) %copy-start.1) | copy-done | bytes 589848
  4.2 0.0 copy-start.2
  4.2 0.7 copy-done.2
  4.9 85.0 %shard_map.68 = (f32[32,512]{1,0:T(8,128)S(1)}, f32[32,512]{1,0:T(8,128)S(1)}) custom-call(bf16[2,8,64,512]{3,2,1,0:T(8,128)(2,1)S(1)} %copy-done, f32[2,8,64]{2,1,0:T(8,128)S(1)} %copy-done.2, f32[1]{0:T(128)S(6)} %copy.9.low, f32[1]{0:T(128)S(6)} %copy.10.high, bf16[1152,256]{1,0:T(8,128)(2,1)S(1)} %copy-done.1), custom_call_target="tpu_custom_call" | custom-call | tf_op jit(solution)/shard_map/pallas_call | solution.py:409
  89.9 0.6 copy.11
  90.5 0.6 copy.12
Async XLA Ops:
  1.9 1.2 %copy-start = (bf16[2,8,64,512]{3,2,1,0:T(8,128)(2,1)S(1)}, bf16[2,8,64,512]{3,2,1,0:T(8,128)(2,1)}, u32[]{:S(2)}) copy-start(bf16[2,8,64,512]{3,2,1,0:T(8,128)(2,1)} %wave.1) | copy-start | bytes 3145732
  3.1 1.1 %copy-start.1 = (bf16[1152,256]{1,0:T(8,128)(2,1)S(1)}, bf16[1152,256]{1,0:T(8,128)(2,1)}, u32[]{:S(2)}) copy-start(bf16[1152,256]{1,0:T(8,128)(2,1)} %constant.2.clone.w_in) | copy-start | bytes 1769476
  4.2 0.7 copy-start.2

commit v2 on v1

v2 whole, which is shorter than its diff:
```python
import functools

import jax
import jax.numpy as jnp
import numpy as np
from jax import lax
from jax.experimental import pallas as pl
from jax.experimental.pallas import tpu as pltpu
from jax.sharding import PartitionSpec as P

MESH = pl.DeviceIdType.MESH
F32, BF16 = jnp.float32, jnp.bfloat16
GROUP = 32
NT = (((1,), (1,)), ((), ()))


def stencil_matrix():
    my, ky = np.zeros((4, 6)), np.zeros((4, 6))
    for i in range(4):
        my[i, i : i + 3] = 1, 4, 1
        ky[i, i : i + 3] = -1, 2, -1
    mz, kz = np.zeros((64, 64)), np.zeros((64, 64))
    for i in range(64):
        for j in range(max(i - 1, 0), min(i + 2, 64)):
            mz[i, j] = 4 if i == j else 1
            kz[i, j] = 2 if i == j else -1
    m = np.einsum("ij,kl->jlik", my, mz).reshape(6, 64, 256)
    g = np.einsum("ij,kl->jlik", ky, mz) + np.einsum("ij,kl->jlik", my, kz)
    g = g.reshape(6, 64, 256)
    p, q = 2 * m + 4 * g, g - m
    own = lambda t: t[1:5].reshape(256, 256)
    edge = lambda t: np.concatenate([t[5], t[0]], axis=0)
    return np.concatenate([own(p), own(q), own(q), edge(p), edge(q), edge(q)], axis=0)


def kernel(
    wave_hbm, pot_hbm, low, high, w_hbm, margin, projected,
    wave, pot, w_in, t, u0, u1, u2, u3, u4, img, d0, rf, ri, gm, part, other, half, rs, ob,
    load, in_s, in_r, pin_s, pin_r, hal_s, hal_r, phal_s, phal_r, edge_s, edge_r,
    f_s, f_r, i_s, i_r, core_s, core_r, rs_s, rs_r, ag_s, ag_r,
):
    loads = [
        pltpu.make_async_copy(src, dst, load.at[i])
        for i, (src, dst) in enumerate([(wave_hbm, wave), (pot_hbm, pot), (w_hbm, w_in)])
    ]
    for copy in loads:
        copy.start()

    sx, sy = lax.axis_index("sx"), lax.axis_index("sy")
    rem, div = lax.rem, lax.div
    xl, z, yy, s4 = div(sx, 4), rem(sx, 4), div(sy, 4), rem(sy, 4)
    xh, c = div(s4, 2), rem(s4, 2)
    x = 2 * xh + xl
    j = sx * 4 + s4

    turn = [None, 1 + 2 * c, 2, 3 - 2 * c]
    zs = [z] + [rem(z + turn[d], 4) for d in (1, 2, 3)]
    xt = [x] + [rem(x + turn[d], 4) for d in (1, 2, 3)]
    ys = [yy] + [rem(yy + turn[d], 4) for d in (1, 2, 3)]
    xls, xhs, cs = [rem(v, 2) for v in xt], [div(v, 2) for v in xt], [c, 1 - c]
    zback = [[z] + [rem(z + 4 - turn_, 4) for turn_ in tt] for tt in (
        (1 + 2 * c, 2, 3 - 2 * c), (3 - 2 * c, 2, 1 + 2 * c))]
    xback = [[x] + [rem(x + 4 - turn_, 4) for turn_ in tt] for tt in (
        (1 + 2 * c, 2, 3 - 2 * c), (3 - 2 * c, 2, 1 + 2 * c))]

    def peer(k):
        dz, dx, dc = k % 4, (k // 4) % 4, k // 16
        return xls[dx] * 4 + zs[dz], xhs[dx] * 2 + cs[dc]

    def source(k):
        dz, dx, dc = k % 4, (k // 4) % 4, k // 16
        zz, xx = zback[dc][dz], xback[dc][dx]
        return rem(xx, 2) * 4 + zz, div(xx, 2) * 2 + cs[dc]

    def remote(src, dst, ss, rr, dev):
        return pltpu.make_async_remote_copy(
            src_ref=src, dst_ref=dst, send_sem=ss, recv_sem=rr, device_id=dev, device_id_type=MESH
        )

    sibling = (sx, sy + 1 - 2 * c)

    def bulk(ref, sem):
        return remote(ref, ref, sem, sem, sibling)

    for u in (u0, u1, u2, u3, u4):
        u[0] = jnp.zeros(u.shape[1:], BF16)
        u[17] = jnp.zeros(u.shape[1:], BF16)
        for b in (0, 1, 10, 11):
            u[:, b] = jnp.zeros((18, 16, 256), BF16)
    d0[:, 0] = jnp.zeros((16, 1, 256), F32)
    d0[:, 9] = jnp.zeros((16, 1, 256), F32)

    barrier = pltpu.get_barrier_semaphore()

    for k in range(1, GROUP):
        px, p4 = peer(k)
        pl.semaphore_signal(barrier, inc=1, device_id=(px, yy * 4 + p4), device_id_type=MESH)
    for dy in (1, 2, 3):
        pl.semaphore_signal(barrier, inc=1, device_id=(sx, ys[dy] * 4 + s4), device_id_type=MESH)

    eye = (
        lax.broadcasted_iota(jnp.int32, (256, 256), 0)
        == lax.broadcasted_iota(jnp.int32, (256, 256), 1)
    ).astype(F32).astype(BF16)
    loads[0].wait()
    loads[1].wait()
    for a in range(2):
        for b in range(2):
            nodes = wave[a, 4 * b : 4 * b + 4].reshape(256, 512)
            for h in range(2):
                t[a, b, 256 * h : 256 * h + 256] = lax.dot_general(
                    eye, nodes[:, 256 * h : 256 * h + 256], NT, preferred_element_type=F32
                ).astype(BF16)
            d0[2 * sx + a, 1 + 2 * s4 + b] = jnp.concatenate(
                [pot[a, 4 * b + i : 4 * b + i + 1, :] for i in range(4)], axis=1
            )

    pl.semaphore_wait(barrier, GROUP - 1 + 3)

    xs = pl.ds(1 + 2 * sx, 2)
    bs = pl.ds(2 + 2 * s4, 2)
    own_pot = d0.at[pl.ds(2 * sx, 2), pl.ds(1 + 2 * s4, 2)]

    def cols(i):
        return pl.ds(pl.multiple_of(16 * i, 16), 16)

    def in_copy(k):
        px, p4 = peer(k)
        return remote(
            t.at[:, :, cols(px * 4 + p4)], u0.at[xs, bs], in_s.at[0], in_r.at[k], (px, yy * 4 + p4)
        )

    for k in range(1, GROUP):
        px, p4 = peer(k)
        remote(own_pot, own_pot, pin_s.at[0], pin_r.at[0], (px, yy * 4 + p4)).start()
    for k in range(1, GROUP):
        in_copy(k).start()

    u0[xs, bs] = t[:, :, cols(j)]

    def edge_ends(side):
        far = rem(yy + 3 + 2 * side, 4)
        return ((2, 10) if side == 0 else (9, 1)) + ((sx, far * 4 + s4),)

    def send_on(s, quarter):
        def send(side):
            mine, theirs, dev = edge_ends(side)
            ux = pl.ds(1 + 2 * s, 2)
            remote(u0.at[ux, mine], u0.at[ux, theirs], hal_s.at[side], hal_r.at[side], dev).start()

        @pl.when(jnp.logical_and(quarter == 0, yy > 0))
        def _():
            send(0)

        @pl.when(jnp.logical_and(quarter == 3, yy < 3))
        def _():
            send(1)

    def pot_edge(side):
        mine, theirs, dev = edge_ends(side)
        return remote(
            d0.at[:, mine - 1], d0.at[:, theirs - 1], phal_s.at[side], phal_r.at[side], dev
        )

    bulk(rs.at[0, 1:GROUP], pin_r.at[0]).wait_recv()

    @pl.when(yy > 0)
    def _():
        pot_edge(0).start()

    @pl.when(yy < 3)
    def _():
        pot_edge(1).start()

    send_on(sx, s4)
    for k in range(1, GROUP):
        in_copy(k).wait_recv()
        send_on(*source(k))

    loads[2].wait()
    centre = 0.5 * (high[0] + low[0])
    inv_radius = 1.0 / (0.5 * (high[0] - low[0]))

    def stencil(u, x0, lo, hi):
        n = hi - lo
        rows = 4 * n * 16
        own, edge = [], []
        for dx in (1, 0, 2):
            px = pl.ds(x0 + dx, 4)
            own.append(u[px, lo:hi].reshape(rows, 256))
            nxt = u[px, lo + 1 : hi + 1, :, 0:128].reshape(rows, 128)
            prv = u[px, lo - 1 : hi - 1, :, 128:256].reshape(rows, 128)
            first = lax.broadcasted_iota(jnp.int32, (rows, 128), 1) < 64
            edge.append(jnp.where(first, nxt, prv))
        lhs = jnp.concatenate(own + edge, axis=1)
        acc = jnp.dot(lhs, w_in[...], preferred_element_type=F32)
        return acc.reshape(4, n, 16, 256)

    def apply_step(u, prev, out, lo, hi):
        @pl.loop(0, 4)
        def _(i):
            x0 = 4 * i
            acc = stencil(u, x0, lo, hi)
            px = pl.ds(x0 + 1, 4)
            v = u[px, lo:hi].astype(F32)
            d = (d0[pl.ds(x0, 4), lo - 1 : hi - 1] - centre) * inv_radius
            if prev is None:
                res = acc * (inv_radius / 72.0) + d * v
            else:
                res = acc * (inv_radius / 36.0) + (2.0 * d) * v - prev[px, lo:hi].astype(F32)
            out[px, lo:hi] = res.astype(BF16)

    def outside_zero(out):
        @pl.when(yy == 0)
        def _():
            out[:, 1] = jnp.zeros((18, 16, 256), BF16)

        @pl.when(yy == 3)
        def _():
            out[:, 10] = jnp.zeros((18, 16, 256), BF16)

    apply_step(u0, None, u1, 3, 9)

    def halo_wait(side):
        bulk(u0.at[1:17, 2], hal_r.at[side]).wait_recv()
        pot_edge(side).wait_recv()

    @pl.when(yy < 3)
    def _():
        halo_wait(0)

    @pl.when(yy > 0)
    def _():
        halo_wait(1)

    apply_step(u0, None, u1, 1, 3)
    apply_step(u0, None, u1, 9, 11)
    outside_zero(u1)
    apply_step(u1, u0, u2, 1, 11)
    outside_zero(u2)
    apply_step(u2, u1, u3, 1, 11)
    outside_zero(u3)
    apply_step(u3, u2, u4, 2, 10)

    def layer(side):
        far = rem(yy + 3 + 2 * side, 4)
        mine, theirs, lanes = (2, 10, pl.ds(0, 128)) if side == 0 else (9, 1, pl.ds(128, 128))
        return remote(
            u4.at[pl.ds(1, 16), mine, :, lanes],
            u4.at[pl.ds(1, 16), theirs, :, lanes],
            edge_s.at[side], edge_r.at[side], (sx, far * 4 + s4),
        )

    @pl.when(yy > 0)
    def _():
        layer(0).start()

    @pl.when(yy < 3)
    def _():
        layer(1).start()

    def send_out(src, dst, ss, rr, first):
        for k in range(1, GROUP):
            px, p4 = peer(k)
            remote(
                src.at[pl.ds(first + 2 * px, 2), pl.ds(2 * first + 2 * p4, 2)],
                dst.at[:, :, cols(j)], ss.at[0], rr.at[0], (px, yy * 4 + p4),
            ).start()

    send_out(u4, rf, f_s, f_r, 1)
    rf[:, :, cols(j)] = u4[xs, bs]

    @pl.when(yy < 3)
    def _():
        layer(0).wait_recv()

    @pl.when(yy > 0)
    def _():
        layer(1).wait_recv()

    @pl.loop(0, 4)
    def _(i):
        x0 = 4 * i
        acc = stencil(u4, x0, 2, 10)
        v = u4[pl.ds(x0 + 1, 4), 2:10].astype(F32)
        res = acc * (1.0 / 72.0) + d0[pl.ds(x0, 4), 1:9] * v
        img[pl.ds(x0, 4)] = res.astype(BF16)

    send_out(img, ri, i_s, i_r, 0)
    ri[:, :, cols(j)] = img[pl.ds(2 * sx, 2), pl.ds(2 * s4, 2)]

    def core_copy(n):
        return remote(
            part.at[n, :, 1 - c], other.at[n], core_s.at[n], core_r.at[n], sibling
        )

    def gram(n, right):
        whole = jnp.concatenate([rf[a, b] for a in range(2) for b in range(2)], axis=1)
        with_ = jnp.concatenate([right[a, b] for a in range(2) for b in range(2)], axis=1)
        for r in range(4):
            g = lax.dot_general(
                whole[128 * r : 128 * r + 128], with_, NT, preferred_element_type=F32
            ).reshape(2, 2, 2, 16, 512)
            gm[2 * r : 2 * r + 2] = g
            part[n, 2 * r : 2 * r + 2] = g.astype(BF16)
        core_copy(n).start()

    def rs_copy(n, k):
        dz, dx, dy = k % 4, (k // 4) % 4, k // 16
        m, h, q = ys[dy] * 2 + xhs[dx], xls[dx], zs[dz]
        return remote(
            half.at[n, m, h, :, pl.ds(pl.multiple_of(128 * q, 128), 128)],
            rs.at[n, k], rs_s.at[n], rs_r.at[n], (h * 4 + q, m * 2 + c),
        )

    def scatter(n):
        core_copy(n).wait_recv()
        half[n] = (gm[:, c] + other[n].astype(F32)).astype(BF16)

        for k in range(1, 64):
            rs_copy(n, k).start()

        rs[n, 0] = half[n, 2 * yy + xh, xl, :, pl.ds(pl.multiple_of(128 * z, 128), 128)]

    def collect(n):
        bulk(rs.at[n, 1:64], rs_r.at[n]).wait_recv()
        ob[sx, n] = jnp.sum(rs[n].astype(F32), axis=0) * (1.0 / 131072.0)

    bulk(t.at[:, :, 0:496], f_r.at[0]).wait_recv()
    gram(0, rf)
    scatter(0)

    bulk(t.at[:, :, 0:496], i_r.at[0]).wait_recv()
    gram(1, ri)
    scatter(1)
    collect(0)
    collect(1)

    for k in range(1, 8):
        far = rem(sx + k, 8)
        remote(ob.at[sx], ob.at[sx], ag_s.at[0], ag_r.at[0], (far, sy)).start()

    for sem in (in_s, f_s, i_s):
        bulk(t.at[:, :, 0:496], sem.at[0]).wait_send()
    bulk(rs.at[0, 1:GROUP], pin_s.at[0]).wait_send()

    def sent(side):
        bulk(u0.at[1:17, 2], hal_s.at[side]).wait_send()
        pot_edge(side).wait_send()
        layer(side).wait_send()

    @pl.when(yy > 0)
    def _():
        sent(0)

    @pl.when(yy < 3)
    def _():
        sent(1)

    for n in range(2):
        core_copy(n).wait_send()
        bulk(rs.at[n, 1:64], rs_s.at[n]).wait_send()
    bulk(ob.at[0:7], ag_s.at[0]).wait_send()
    bulk(ob.at[0:7], ag_r.at[0]).wait_recv()
    for s in range(8):
        rows, lanes = pl.ds(16 * (s // 4), 16), pl.ds(128 * (s % 4), 128)
        margin[rows, lanes] = ob[s, 0]
        projected[rows, lanes] = ob[s, 1]


def on_device(wave, potential, lower_cut, upper_edge):
    dma = pltpu.SemaphoreType.DMA
    field = pltpu.VMEM((18, 12, 16, 256), BF16)
    block = pltpu.VMEM((2, 2, 512, 256), BF16)
    vmem = pl.BlockSpec(memory_space=pltpu.VMEM)
    hbm = pl.BlockSpec(memory_space=pl.ANY)
    smem = pl.BlockSpec(memory_space=pltpu.SMEM)
    weights = jnp.asarray(stencil_matrix(), BF16)
    return pl.pallas_call(
        kernel,
        out_shape=[jax.ShapeDtypeStruct((32, 512), F32)] * 2,
        in_specs=[hbm, hbm, smem, smem, hbm],
        out_specs=[vmem, vmem],
        scratch_shapes=[
            pltpu.VMEM(wave.shape, BF16),
            pltpu.VMEM(potential.shape, F32),
            pltpu.VMEM(weights.shape, BF16),
            block,
            field, field, field, field, field,
            pltpu.VMEM((16, 8, 16, 256), BF16),
            pltpu.VMEM((16, 10, 1, 256), F32),
            block, block,
            pltpu.VMEM((8, 2, 2, 16, 512), F32),
            pltpu.VMEM((2, 8, 2, 2, 16, 512), BF16),
            pltpu.VMEM((2, 8, 2, 16, 512), BF16),
            pltpu.VMEM((2, 8, 2, 16, 512), BF16),
            pltpu.VMEM((2, 64, 16, 128), BF16),
            pltpu.VMEM((8, 2, 16, 128), F32),
            dma((3,)), dma((1,)), dma((32,)), dma((1,)), dma((1,)),
            dma((2,)), dma((2,)), dma((2,)), dma((2,)),
            dma((2,)), dma((2,)),
            dma((1,)), dma((1,)), dma((1,)), dma((1,)),
            dma((2,)), dma((2,)), dma((2,)), dma((2,)),
            dma((1,)), dma((1,)),
        ],
        compiler_params=pltpu.CompilerParams(
            collective_id=0, has_side_effects=True, vmem_limit_bytes=127 << 19
        ),
    )(wave, potential, lower_cut, upper_edge, weights)


def solution(mesh):
    return jax.shard_map(
        on_device,
        mesh=mesh,
        in_specs=(P("sx", "sy", None, None), P("sx", "sy", None), P(), P()),
        out_specs=(P("sy", None), P("sy", None)),
        check_vma=False,
    )
```

time: 91.4 us -> 82.2 us (0.90)
  Pallas kernels: 85 us -> 77.9 us
  local copies, waits for them, and re-layouts: 4.24 us -> 2.14 us
    pallas_call x1, Pallas kernels: 85 us -> 77.9 us  [on_device(): pl.pallas_call(kernel, out_shape=[jax.ShapeDtypeStruct((32, 512), F32)] *...]
    unnamed x8 -> x4, local copies, waits for them, and re-layouts: 4.24 us -> 2.14 us
where the time goes in v2:
time: 82.2 us; the launch traced here: 82 us
  Pallas kernels  77.9 us (95%)
  local copies, waits for them, and re-layouts  2.14 us (3%)
  between operations  1.94 us (2%)
    pallas_call x1, Pallas kernels, on_device(): pl.pallas_call(kernel, out_shape=[jax.ShapeDtypeStruct((32, 512), F32)] *...  77.9 us
    unnamed x4, local copies, waits for them, and re-layouts  2.14 us

profile of v2, /device:TPU:1, one launch (start us, length us, event | category | flops | bytes accessed | tf_op | source)
XLA Modules:
  0.0 82.0 jit_solution(10274445271891402075)
XLA Ops:
  1.9 77.9 %shard_map.68 = (f32[32,512]{1,0:T(8,128)}, f32[32,512]{1,0:T(8,128)}) custom-call(bf16[2,8,64,512]{3,2,1,0:T(8,128)(2,1)} %wave_hbm.1, f32[2,8,64]{2,1,0:T(8,128)} %pot_hbm.1, f32[1]{0:T(128)S(6)} %copy.9.low, f32[1]{0:T(128)S(6)} %copy.10.high, bf16[1152,256]{1,0:T(8,128)(2,1)} %constant.2.clone.w_hbm), custom_call_target="tpu_custom_call" | custom-call | tf_op jit(solution)/shard_map/pallas_call | solution.py:379
  79.8 0.0 copy-start
  79.8 1.5 %copy.11 = f32[32,512]{1,0:T(8,128)} copy(f32[32,512]{1,0:T(8,128)} %get-tuple-element.4) | data formatting | bytes 131072
  81.3 0.0 copy-done
  81.3 0.6 copy.12
Async XLA Ops:
  79.8 1.5 %copy-start = (f32[32,512]{1,0:T(8,128)S(1)}, f32[32,512]{1,0:T(8,128)}, u32[]{:S(2)}) copy-start(f32[32,512]{1,0:T(8,128)} %get-tuple-element.5) | copy-start | bytes 196612

commit v3 on v2

--- a/solution.py
+++ b/solution.py
@@ -11,6 +11,9 @@
 MESH = pl.DeviceIdType.MESH
 F32, BF16 = jnp.float32, jnp.bfloat16
 GROUP = 32
+FIRST = (2, 8)
+PLANE = (10, 6, 14, 9, 11, 5, 7, 13, 15, 1, 3, 4, 12)
+OTHER = (26, 22, 30, 25, 27, 18, 24, 21, 23, 29, 31, 17, 19, 20, 28, 16)
 NT = (((1,), (1,)), ((), ()))
 
 
@@ -30,14 +33,14 @@
     p, q = 2 * m + 4 * g, g - m
     own = lambda t: t[1:5].reshape(256, 256)
     edge = lambda t: np.concatenate([t[5], t[0]], axis=0)
-    return np.concatenate([own(p), own(q), own(q), edge(p), edge(q), edge(q)], axis=0)
+    return np.concatenate([own(p), own(q), edge(p), edge(q)], axis=0)
 
 
 def kernel(
     wave_hbm, pot_hbm, low, high, w_hbm, margin, projected,
-    wave, pot, w_in, t, u0, u1, u2, u3, u4, img, d0, rf, ri, gm, part, other, half, rs, ob,
+    wave, pot, w_in, t, u0, u1, u2, u3, u4, co, ce, d0, rf, rco, rce, loc, ri, gm, part, other, half, rs, ob,
     load, in_s, in_r, pin_s, pin_r, hal_s, hal_r, phal_s, phal_r, edge_s, edge_r,
-    f_s, f_r, i_s, i_r, core_s, core_r, rs_s, rs_r, ag_s, ag_r,
+    f_s, f_r, i_s, i_r, core_s, core_r, rs_s, rs_r, ag_s, ag_r, plane, chip,
 ):
     loads = [
         pltpu.make_async_copy(src, dst, load.at[i])
@@ -91,12 +94,10 @@
     d0[:, 9] = jnp.zeros((16, 1, 256), F32)
 
     barrier = pltpu.get_barrier_semaphore()
-
-    for k in range(1, GROUP):
-        px, p4 = peer(k)
-        pl.semaphore_signal(barrier, inc=1, device_id=(px, yy * 4 + p4), device_id_type=MESH)
-    for dy in (1, 2, 3):
-        pl.semaphore_signal(barrier, inc=1, device_id=(sx, ys[dy] * 4 + s4), device_id_type=MESH)
+    direct = [(px, yy * 4 + p4) for px, p4 in (peer(k) for k in (1, 2, 3, 4, 8, 12, 16))]
+    direct += [(sx, ys[dy] * 4 + s4) for dy in (1, 2, 3)]
+    for dev in direct:
+        pl.semaphore_signal(barrier, inc=1, device_id=dev, device_id_type=MESH)
 
     eye = (
         lax.broadcasted_iota(jnp.int32, (256, 256), 0)
@@ -108,35 +109,43 @@
         for b in range(2):
             nodes = wave[a, 4 * b : 4 * b + 4].reshape(256, 512)
             for h in range(2):
-                t[a, b, 256 * h : 256 * h + 256] = lax.dot_general(
+                turned = lax.dot_general(
                     eye, nodes[:, 256 * h : 256 * h + 256], NT, preferred_element_type=F32
-                ).astype(BF16)
+                )
+                t[16 * h : 16 * h + 16, a, b] = turned.astype(BF16).reshape(16, 16, 256)
             d0[2 * sx + a, 1 + 2 * s4 + b] = jnp.concatenate(
                 [pot[a, 4 * b + i : 4 * b + i + 1, :] for i in range(4)], axis=1
             )
 
-    pl.semaphore_wait(barrier, GROUP - 1 + 3)
+    pl.semaphore_wait(barrier, len(direct))
 
     xs = pl.ds(1 + 2 * sx, 2)
     bs = pl.ds(2 + 2 * s4, 2)
     own_pot = d0.at[pl.ds(2 * sx, 2), pl.ds(1 + 2 * s4, 2)]
 
-    def cols(i):
-        return pl.ds(pl.multiple_of(16 * i, 16), 16)
-
     def in_copy(k):
         px, p4 = peer(k)
         return remote(
-            t.at[:, :, cols(px * 4 + p4)], u0.at[xs, bs], in_s.at[0], in_r.at[k], (px, yy * 4 + p4)
-        )
-
-    for k in range(1, GROUP):
+            t.at[px * 4 + p4], u0.at[xs, bs], in_s.at[0], in_r.at[k], (px, yy * 4 + p4)
+        )
+
+    def send_in(ks):
+        for k in ks:
+            px, p4 = peer(k)
+            remote(own_pot, own_pot, pin_s.at[0], pin_r.at[0], (px, yy * 4 + p4)).start()
+            in_copy(k).start()
+
+    for k in (1, 2, 3):
         px, p4 = peer(k)
-        remote(own_pot, own_pot, pin_s.at[0], pin_r.at[0], (px, yy * 4 + p4)).start()
-    for k in range(1, GROUP):
-        in_copy(k).start()
-
-    u0[xs, bs] = t[:, :, cols(j)]
+        pl.semaphore_signal(plane, inc=1, device_id=(px, yy * 4 + p4), device_id_type=MESH)
+    send_in(FIRST)
+    pl.semaphore_wait(plane, 3)
+    pl.semaphore_signal(chip, inc=1, device_id=sibling, device_id_type=MESH)
+    send_in(PLANE)
+    pl.semaphore_wait(chip, 1)
+    send_in(OTHER)
+
+    u0[xs, bs] = t[j]
 
     def edge_ends(side):
         far = rem(yy + 3 + 2 * side, 4)
@@ -173,7 +182,7 @@
         pot_edge(1).start()
 
     send_on(sx, s4)
-    for k in range(1, GROUP):
+    for k in (*FIRST, *PLANE, *OTHER):
         in_copy(k).wait_recv()
         send_on(*source(k))
 
@@ -181,34 +190,37 @@
     centre = 0.5 * (high[0] + low[0])
     inv_radius = 1.0 / (0.5 * (high[0] - low[0]))
 
+    def edge_slab(nxt, prv):
+        return jnp.where(lax.broadcasted_iota(jnp.int32, nxt.shape, len(nxt.shape) - 1) < 64, nxt, prv)
+
     def stencil(u, x0, lo, hi):
         n = hi - lo
         rows = 4 * n * 16
-        own, edge = [], []
-        for dx in (1, 0, 2):
-            px = pl.ds(x0 + dx, 4)
-            own.append(u[px, lo:hi].reshape(rows, 256))
-            nxt = u[px, lo + 1 : hi + 1, :, 0:128].reshape(rows, 128)
-            prv = u[px, lo - 1 : hi - 1, :, 128:256].reshape(rows, 128)
-            first = lax.broadcasted_iota(jnp.int32, (rows, 128), 1) < 64
-            edge.append(jnp.where(first, nxt, prv))
-        lhs = jnp.concatenate(own + edge, axis=1)
-        acc = jnp.dot(lhs, w_in[...], preferred_element_type=F32)
+        mid = u[pl.ds(x0 + 1, 4), lo - 1 : hi + 1]
+        beside = u[pl.ds(x0, 4), lo - 1 : hi + 1] + u[pl.ds(x0 + 2, 4), lo - 1 : hi + 1]
+        slabs = [v[:, 1 : n + 1].reshape(rows, 256) for v in (mid, beside)]
+        slabs += [
+            edge_slab(v[:, 2:, :, 0:128], v[:, :n, :, 128:256]).reshape(rows, 128)
+            for v in (mid, beside)
+        ]
+        acc = jnp.dot(jnp.concatenate(slabs, axis=1), w_in[...], preferred_element_type=F32)
         return acc.reshape(4, n, 16, 256)
 
+    def apply_chunk(u, prev, out, x0, lo, hi):
+        acc = stencil(u, x0, lo, hi)
+        px = pl.ds(x0 + 1, 4)
+        v = u[px, lo:hi].astype(F32)
+        d = (d0[pl.ds(x0, 4), lo - 1 : hi - 1] - centre) * inv_radius
+        if prev is None:
+            res = acc * (inv_radius / 72.0) + d * v
+        else:
+            res = acc * (inv_radius / 36.0) + (2.0 * d) * v - prev[px, lo:hi].astype(F32)
+        out[px, lo:hi] = res.astype(BF16)
+
     def apply_step(u, prev, out, lo, hi):
-        @pl.loop(0, 4)
+        @pl.loop(0, 4, unroll=4)
         def _(i):
-            x0 = 4 * i
-            acc = stencil(u, x0, lo, hi)
-            px = pl.ds(x0 + 1, 4)
-            v = u[px, lo:hi].astype(F32)
-            d = (d0[pl.ds(x0, 4), lo - 1 : hi - 1] - centre) * inv_radius
-            if prev is None:
-                res = acc * (inv_radius / 72.0) + d * v
-            else:
-                res = acc * (inv_radius / 36.0) + (2.0 * d) * v - prev[px, lo:hi].astype(F32)
-            out[px, lo:hi] = res.astype(BF16)
+            apply_chunk(u, prev, out, 4 * i, lo, hi)
 
     def outside_zero(out):
         @pl.when(yy == 0)
@@ -260,15 +272,15 @@
         layer(1).start()
 
     def send_out(src, dst, ss, rr, first):
-        for k in range(1, GROUP):
+        for k in (*OTHER, *PLANE, *FIRST):
             px, p4 = peer(k)
             remote(
                 src.at[pl.ds(first + 2 * px, 2), pl.ds(2 * first + 2 * p4, 2)],
-                dst.at[:, :, cols(j)], ss.at[0], rr.at[0], (px, yy * 4 + p4),
+                dst.at[j], ss.at[0], rr.at[0], (px, yy * 4 + p4),
             ).start()
 
     send_out(u4, rf, f_s, f_r, 1)
-    rf[:, :, cols(j)] = u4[xs, bs]
+    rf[j] = u4[xs, bs]
 
     @pl.when(yy < 3)
     def _():
@@ -278,32 +290,80 @@
     def _():
         layer(1).wait_recv()
 
-    @pl.loop(0, 4)
+    zero = jnp.zeros((), BF16)
+
+    @pl.loop(0, 2)
     def _(i):
-        x0 = 4 * i
-        acc = stencil(u4, x0, 2, 10)
-        v = u4[pl.ds(x0 + 1, 4), 2:10].astype(F32)
-        res = acc * (1.0 / 72.0) + d0[pl.ds(x0, 4), 1:9] * v
-        img[pl.ds(x0, 4)] = res.astype(BF16)
-
-    send_out(img, ri, i_s, i_r, 0)
-    ri[:, :, cols(j)] = img[pl.ds(2 * sx, 2), pl.ds(2 * s4, 2)]
+        own, slab_p, slab_q, even_p, even_q = [], [], [], [], []
+        first = lax.broadcasted_iota(jnp.int32, (8, 16, 128), 2) < 64
+        last = lax.broadcasted_iota(jnp.int32, (8, 16, 128), 0) % 2 == 1
+        for m in range(4):
+            before, here, after = (u4.at[8 * i + 2 * m + n] for n in (1, 2, 3))
+            own.append(after[2:10].reshape(128, 256))
+            nxt = [u[3:11, :, 0:128] for u in (before, here, after)]
+            slab_p.append(jnp.where(first & last, nxt[1], zero).reshape(128, 128))
+            far = nxt[2] + jnp.where(last, nxt[0], zero)
+            slab_q.append(jnp.where(first, far, after[1:9, :, 128:256]).reshape(128, 128))
+            for b in (4, 6, 8, 10):
+                even_p.append(jnp.where(first[0], before[b, :, 0:128], zero))
+                even_q.append(jnp.where(first[0], here[b, :, 0:128], zero))
+        join = lambda parts: jnp.concatenate(parts, axis=0)
+        lhs = jnp.concatenate([join(own), join(slab_p), join(slab_q)], axis=1)
+        acc = jnp.dot(lhs, w_in[256:768], preferred_element_type=F32) * (2.0 / 72.0)
+        co[pl.ds(4 * i, 4)] = acc.astype(BF16).reshape(4, 8, 16, 256)
+        lhs = jnp.concatenate([join(even_p), join(even_q)], axis=1)
+        acc = jnp.dot(lhs, w_in[512:768, 128:256], preferred_element_type=F32) * (2.0 / 72.0)
+        ce[pl.ds(4 * i, 4)] = acc.astype(BF16).reshape(4, 4, 16, 128)
+
+    for k in (*OTHER, *PLANE, *FIRST):
+        px, p4 = peer(k)
+        dev = (px, yy * 4 + p4)
+        remote(co.at[px, pl.ds(2 * p4, 2)], rco.at[j], i_s.at[0], i_r.at[0], dev).start()
+        remote(ce.at[px, p4], rce.at[j], i_s.at[1], i_r.at[1], dev).start()
+    rco[j] = co[sx, pl.ds(2 * s4, 2)]
+    rce[j] = ce[sx, s4]
 
     def core_copy(n):
         return remote(
             part.at[n, :, 1 - c], other.at[n], core_s.at[n], core_r.at[n], sibling
         )
 
-    def gram(n, right):
-        whole = jnp.concatenate([rf[a, b] for a in range(2) for b in range(2)], axis=1)
-        with_ = jnp.concatenate([right[a, b] for a in range(2) for b in range(2)], axis=1)
+    units = [(a, b) for a in range(2) for b in range(2)]
+
+    def flat(ref):
+        return ref.reshape(512, ref.shape[-1])
+
+    def gram(n, left, right):
         for r in range(4):
             g = lax.dot_general(
-                whole[128 * r : 128 * r + 128], with_, NT, preferred_element_type=F32
+                left[128 * r : 128 * r + 128], right, NT, preferred_element_type=F32
             ).reshape(2, 2, 2, 16, 512)
             gm[2 * r : 2 * r + 2] = g
             part[n, 2 * r : 2 * r + 2] = g.astype(BF16)
         core_copy(n).start()
+
+    def local_image():
+        first = lax.broadcasted_iota(jnp.int32, (512, 128), 1) < 64
+        for a, b in units:
+            slabs = [flat(rf[:, n, b]) for n in (a, 1 - a)]
+            for n in (a, 1 - a):
+                if b == 0:
+                    slabs.append(jnp.where(first, flat(rf[:, n, 1, :, 0:128]), zero))
+                else:
+                    slabs.append(jnp.where(first, zero, flat(rf[:, n, 0, :, 128:256])))
+            acc = jnp.dot(jnp.concatenate(slabs, axis=1), w_in[...], preferred_element_type=F32)
+            here = d0[2 * sx + a, 1 + 2 * s4 + b] * flat(rf[:, a, b]).astype(F32)
+            loc[a, b] = acc * (1.0 / 72.0) + here
+
+    def whole_image():
+        for a, b in units:
+            full = loc[a, b]
+            if a == 1:
+                full += flat(rco[:, b]).astype(F32)
+            elif b == 1:
+                far = flat(rce[...]).astype(F32)
+                full += jnp.concatenate([jnp.zeros((512, 128), F32), far], axis=1)
+            ri[a, b] = full.astype(BF16)
 
     def rs_copy(n, k):
         dz, dx, dy = k % 4, (k // 4) % 4, k // 16
@@ -324,14 +384,24 @@
 
     def collect(n):
         bulk(rs.at[n, 1:64], rs_r.at[n]).wait_recv()
-        ob[sx, n] = jnp.sum(rs[n].astype(F32), axis=0) * (1.0 / 131072.0)
-
-    bulk(t.at[:, :, 0:496], f_r.at[0]).wait_recv()
-    gram(0, rf)
+        ob[sx, n] = jnp.sum(rs[n].astype(F32), axis=0) * ((1.0 - 0.5 * n) / 131072.0)
+
+    bulk(t.at[1:GROUP], f_r.at[0]).wait_recv()
+    field_rows = jnp.concatenate([flat(rf[:, a, b]) for a, b in units], axis=1)
+    gram(0, field_rows, field_rows)
+    local_image()
     scatter(0)
 
-    bulk(t.at[:, :, 0:496], i_r.at[0]).wait_recv()
-    gram(1, ri)
+    bulk(t.at[1:GROUP, 0], i_r.at[0]).wait_recv()
+    bulk(rs.at[0, 1:GROUP], i_r.at[1]).wait_recv()
+    whole_image()
+    field_rows = [flat(rf[:, a, b]) for a, b in units]
+    image_rows = [ri[a, b] for a, b in units]
+    gram(
+        1,
+        jnp.concatenate(field_rows + image_rows, axis=1),
+        jnp.concatenate(image_rows + field_rows, axis=1),
+    )
     scatter(1)
     collect(0)
     collect(1)
@@ -340,8 +410,10 @@
         far = rem(sx + k, 8)
         remote(ob.at[sx], ob.at[sx], ag_s.at[0], ag_r.at[0], (far, sy)).start()
 
-    for sem in (in_s, f_s, i_s):
-        bulk(t.at[:, :, 0:496], sem.at[0]).wait_send()
+    for sem in (in_s, f_s):
+        bulk(t.at[1:GROUP], sem.at[0]).wait_send()
+    bulk(t.at[1:GROUP, 0], i_s.at[0]).wait_send()
+    bulk(rs.at[0, 1:GROUP], i_s.at[1]).wait_send()
     bulk(rs.at[0, 1:GROUP], pin_s.at[0]).wait_send()
 
     def sent(side):
@@ -371,7 +443,7 @@
 def on_device(wave, potential, lower_cut, upper_edge):
     dma = pltpu.SemaphoreType.DMA
     field = pltpu.VMEM((18, 12, 16, 256), BF16)
-    block = pltpu.VMEM((2, 2, 512, 256), BF16)
+    block = pltpu.VMEM((GROUP, 2, 2, 16, 256), BF16)
     vmem = pl.BlockSpec(memory_space=pltpu.VMEM)
     hbm = pl.BlockSpec(memory_space=pl.ANY)
     smem = pl.BlockSpec(memory_space=pltpu.SMEM)
@@ -387,9 +459,14 @@
             pltpu.VMEM(weights.shape, BF16),
             block,
             field, field, field, field, field,
-            pltpu.VMEM((16, 8, 16, 256), BF16),
+            pltpu.VMEM((8, 8, 16, 256), BF16),
+            pltpu.VMEM((8, 4, 16, 128), BF16),
             pltpu.VMEM((16, 10, 1, 256), F32),
-            block, block,
+            block,
+            pltpu.VMEM((GROUP, 2, 16, 256), BF16),
+            pltpu.VMEM((GROUP, 16, 128), BF16),
+            pltpu.VMEM((2, 2, 512, 256), F32),
+            pltpu.VMEM((2, 2, 512, 256), BF16),
             pltpu.VMEM((8, 2, 2, 16, 512), F32),
             pltpu.VMEM((2, 8, 2, 2, 16, 512), BF16),
             pltpu.VMEM((2, 8, 2, 16, 512), BF16),
@@ -399,9 +476,10 @@
             dma((3,)), dma((1,)), dma((32,)), dma((1,)), dma((1,)),
             dma((2,)), dma((2,)), dma((2,)), dma((2,)),
             dma((2,)), dma((2,)),
-            dma((1,)), dma((1,)), dma((1,)), dma((1,)),
+            dma((1,)), dma((1,)), dma((2,)), dma((2,)),
             dma((2,)), dma((2,)), dma((2,)), dma((2,)),
             dma((1,)), dma((1,)),
+            pltpu.SemaphoreType.REGULAR, pltpu.SemaphoreType.REGULAR,
         ],
         compiler_params=pltpu.CompilerParams(
             collective_id=0, has_side_effects=True, vmem_limit_bytes=127 << 19

time: 82.2 us -> 74.8 us (0.910)
  Pallas kernels: 77.9 us -> 70.5 us
    pallas_call x1, Pallas kernels: 77.9 us -> 70.5 us  [on_device(): pl.pallas_call(kernel, out_shape=[jax.ShapeDtypeStruct((32, 512), F32)] *...]
where the time goes in v3:
time: 74.8 us; the launch traced here: 74.6 us
  Pallas kernels  70.5 us (94%)
  local copies, waits for them, and re-layouts  2.14 us (3%)
  between operations  1.94 us (3%)
    pallas_call x1, Pallas kernels, on_device(): pl.pallas_call(kernel, out_shape=[jax.ShapeDtypeStruct((32, 512), F32)] *...  70.5 us
    unnamed x4, local copies, waits for them, and re-layouts  2.14 us

profile of v3, /device:TPU:1, one launch (start us, length us, event | category | flops | bytes accessed | tf_op | source)
XLA Modules:
  0.0 74.6 jit_solution(7568453698225479256)
XLA Ops:
  1.9 70.5 %shard_map.68 = (f32[32,512]{1,0:T(8,128)}, f32[32,512]{1,0:T(8,128)}) custom-call(bf16[2,8,64,512]{3,2,1,0:T(8,128)(2,1)} %wave_hbm.1, f32[2,8,64]{2,1,0:T(8,128)} %pot_hbm.1, f32[1]{0:T(128)S(6)} %copy.9.low, f32[1]{0:T(128)S(6)} %copy.10.high, bf16[768,256]{1,0:T(8,128)(2,1)} %constant.2.clone.w_hbm), custom_call_target="tpu_custom_call" | custom-call | tf_op jit(solution)/shard_map/pallas_call | solution.py:451
  72.5 0.0 copy-start
  72.5 1.5 %copy.11 = f32[32,512]{1,0:T(8,128)} copy(f32[32,512]{1,0:T(8,128)} %get-tuple-element.4) | data formatting | bytes 131072
  74.0 0.0 copy-done
  74.0 0.6 copy.12
Async XLA Ops:
  72.5 1.5 %copy-start = (f32[32,512]{1,0:T(8,128)S(1)}, f32[32,512]{1,0:T(8,128)}, u32[]{:S(2)}) copy-start(f32[32,512]{1,0:T(8,128)} %get-tuple-element.5) | copy-start | bytes 196612

commit v4 on v3

--- a/solution.py
+++ b/solution.py
@@ -11,8 +11,8 @@
 MESH = pl.DeviceIdType.MESH
 F32, BF16 = jnp.float32, jnp.bfloat16
 GROUP = 32
-FIRST = (2, 8)
-PLANE = (10, 6, 14, 9, 11, 5, 7, 13, 15, 1, 3, 4, 12)
+FIRST = (2, 8, 1, 3, 4, 12)
+PLANE = (10, 6, 14, 9, 11, 5, 7, 13, 15)
 OTHER = (26, 22, 30, 25, 27, 18, 24, 21, 23, 29, 31, 17, 19, 20, 28, 16)
 NT = (((1,), (1,)), ((), ()))
 
@@ -38,9 +38,9 @@
 
 def kernel(
     wave_hbm, pot_hbm, low, high, w_hbm, margin, projected,
-    wave, pot, w_in, t, u0, u1, u2, u3, u4, co, ce, d0, rf, rco, rce, loc, ri, gm, part, other, half, rs, ob,
+    wave, pot, w_in, t, u0, u1, u2, u3, u4, co, ce, d0, rf, rco, rce, ri, gm, part, other, half, ysum, plane_part, rs, ob,
     load, in_s, in_r, pin_s, pin_r, hal_s, hal_r, phal_s, phal_r, edge_s, edge_r,
-    f_s, f_r, i_s, i_r, core_s, core_r, rs_s, rs_r, ag_s, ag_r, plane, chip,
+    f_s, f_r, i_s, i_r, core_s, core_r, y_s, y_r, rs_s, rs_r, ag_s, ag_r, plane, chip,
 ):
     loads = [
         pltpu.make_async_copy(src, dst, load.at[i])
@@ -61,19 +61,9 @@
     xt = [x] + [rem(x + turn[d], 4) for d in (1, 2, 3)]
     ys = [yy] + [rem(yy + turn[d], 4) for d in (1, 2, 3)]
     xls, xhs, cs = [rem(v, 2) for v in xt], [div(v, 2) for v in xt], [c, 1 - c]
-    zback = [[z] + [rem(z + 4 - turn_, 4) for turn_ in tt] for tt in (
-        (1 + 2 * c, 2, 3 - 2 * c), (3 - 2 * c, 2, 1 + 2 * c))]
-    xback = [[x] + [rem(x + 4 - turn_, 4) for turn_ in tt] for tt in (
-        (1 + 2 * c, 2, 3 - 2 * c), (3 - 2 * c, 2, 1 + 2 * c))]
-
     def peer(k):
         dz, dx, dc = k % 4, (k // 4) % 4, k // 16
         return xls[dx] * 4 + zs[dz], xhs[dx] * 2 + cs[dc]
-
-    def source(k):
-        dz, dx, dc = k % 4, (k // 4) % 4, k // 16
-        zz, xx = zback[dc][dz], xback[dc][dx]
-        return rem(xx, 2) * 4 + zz, div(xx, 2) * 2 + cs[dc]
 
     def remote(src, dst, ss, rr, dev):
         return pltpu.make_async_remote_copy(
@@ -126,24 +116,32 @@
     def in_copy(k):
         px, p4 = peer(k)
         return remote(
-            t.at[px * 4 + p4], u0.at[xs, bs], in_s.at[0], in_r.at[k], (px, yy * 4 + p4)
+            t.at[px * 4 + p4], u0.at[xs, bs], in_s.at[0], in_r.at[j], (px, yy * 4 + p4)
         )
 
     def send_in(ks):
         for k in ks:
-            px, p4 = peer(k)
-            remote(own_pot, own_pot, pin_s.at[0], pin_r.at[0], (px, yy * 4 + p4)).start()
             in_copy(k).start()
 
-    for k in (1, 2, 3):
-        px, p4 = peer(k)
-        pl.semaphore_signal(plane, inc=1, device_id=(px, yy * 4 + p4), device_id_type=MESH)
+    def send_pot(strip, stage, devs):
+        for dev in devs:
+            remote(strip, strip, pin_s.at[stage], pin_r.at[stage], dev).start()
+
+    along_z, along_x = direct[0:3], direct[3:6]
+    for dev in along_z:
+        pl.semaphore_signal(plane, inc=1, device_id=dev, device_id_type=MESH)
+    send_pot(own_pot, 0, along_z)
     send_in(FIRST)
     pl.semaphore_wait(plane, 3)
     pl.semaphore_signal(chip, inc=1, device_id=sibling, device_id_type=MESH)
+    bulk(rs.at[0, 0:3], pin_r.at[0]).wait_recv()
+    send_pot(d0.at[pl.ds(8 * xl, 8), pl.ds(1 + 2 * s4, 2)], 1, along_x)
     send_in(PLANE)
     pl.semaphore_wait(chip, 1)
     send_in(OTHER)
+    bulk(rs.at[0, 0:12], pin_r.at[1]).wait_recv()
+    for q in (c, 2 + c):
+        send_pot(d0.at[:, pl.ds(1 + 2 * q, 2)], 2, [sibling])
 
     u0[xs, bs] = t[j]
 
@@ -152,18 +150,13 @@
         return ((2, 10) if side == 0 else (9, 1)) + ((sx, far * 4 + s4),)
 
     def send_on(s, quarter):
-        def send(side):
-            mine, theirs, dev = edge_ends(side)
-            ux = pl.ds(1 + 2 * s, 2)
+        side = quarter // 3
+        mine, theirs, dev = edge_ends(side)
+        ux = pl.ds(1 + 2 * s, 2)
+
+        @pl.when(yy > 0 if side == 0 else yy < 3)
+        def _():
             remote(u0.at[ux, mine], u0.at[ux, theirs], hal_s.at[side], hal_r.at[side], dev).start()
-
-        @pl.when(jnp.logical_and(quarter == 0, yy > 0))
-        def _():
-            send(0)
-
-        @pl.when(jnp.logical_and(quarter == 3, yy < 3))
-        def _():
-            send(1)
 
     def pot_edge(side):
         mine, theirs, dev = edge_ends(side)
@@ -171,7 +164,7 @@
             d0.at[:, mine - 1], d0.at[:, theirs - 1], phal_s.at[side], phal_r.at[side], dev
         )
 
-    bulk(rs.at[0, 1:GROUP], pin_r.at[0]).wait_recv()
+    bulk(rs.at[0, 0:16], pin_r.at[2]).wait_recv()
 
     @pl.when(yy > 0)
     def _():
@@ -181,10 +174,18 @@
     def _():
         pot_edge(1).start()
 
-    send_on(sx, s4)
-    for k in (*FIRST, *PLANE, *OTHER):
-        in_copy(k).wait_recv()
-        send_on(*source(k))
+    def arrived(i):
+        @pl.when(j != i)
+        def _():
+            bulk(u0.at[xs, bs], in_r.at[i]).wait_recv()
+
+    for s in range(8):
+        for quarter in (0, 3):
+            arrived(4 * s + quarter)
+            send_on(s, quarter)
+    for s in range(8):
+        for quarter in (1, 2):
+            arrived(4 * s + quarter)
 
     loads[2].wait()
     centre = 0.5 * (high[0] + low[0])
@@ -309,10 +310,10 @@
                 even_q.append(jnp.where(first[0], here[b, :, 0:128], zero))
         join = lambda parts: jnp.concatenate(parts, axis=0)
         lhs = jnp.concatenate([join(own), join(slab_p), join(slab_q)], axis=1)
-        acc = jnp.dot(lhs, w_in[256:768], preferred_element_type=F32) * (2.0 / 72.0)
+        acc = jnp.dot(lhs, w_in[256:768], preferred_element_type=F32) * (1.0 / 72.0)
         co[pl.ds(4 * i, 4)] = acc.astype(BF16).reshape(4, 8, 16, 256)
         lhs = jnp.concatenate([join(even_p), join(even_q)], axis=1)
-        acc = jnp.dot(lhs, w_in[512:768, 128:256], preferred_element_type=F32) * (2.0 / 72.0)
+        acc = jnp.dot(lhs, w_in[512:768, 128:256], preferred_element_type=F32) * (1.0 / 72.0)
         ce[pl.ds(4 * i, 4)] = acc.astype(BF16).reshape(4, 4, 16, 128)
 
     for k in (*OTHER, *PLANE, *FIRST):
@@ -323,24 +324,25 @@
     rco[j] = co[sx, pl.ds(2 * s4, 2)]
     rce[j] = ce[sx, s4]
 
-    def core_copy(n):
+    units = [(a, b) for a in range(2) for b in range(2)]
+
+    def flat(value):
+        return value.reshape(-1, value.shape[-1])
+
+    def core_copy(n, r):
         return remote(
-            part.at[n, :, 1 - c], other.at[n], core_s.at[n], core_r.at[n], sibling
+            part.at[n, r, :, 1 - c], other.at[n, r], core_s.at[n, r], core_r.at[n, r], sibling
         )
 
-    units = [(a, b) for a in range(2) for b in range(2)]
-
-    def flat(ref):
-        return ref.reshape(512, ref.shape[-1])
-
-    def gram(n, left, right):
-        for r in range(4):
-            g = lax.dot_general(
-                left[128 * r : 128 * r + 128], right, NT, preferred_element_type=F32
-            ).reshape(2, 2, 2, 16, 512)
-            gm[2 * r : 2 * r + 2] = g
-            part[n, 2 * r : 2 * r + 2] = g.astype(BF16)
-        core_copy(n).start()
+    def give(n, r, g):
+        g = g.reshape(2, 2, 2, 16, 512)
+        gm[n, r] = g
+        part[n, r] = g.astype(BF16)
+        core_copy(n, r).start()
+
+    def take(n, r):
+        core_copy(n, r).wait_recv()
+        half[n, r] = (gm[n, r, :, c] + other[n, r].astype(F32)).astype(BF16)
 
     def local_image():
         first = lax.broadcasted_iota(jnp.int32, (512, 128), 1) < 64
@@ -353,58 +355,80 @@
                     slabs.append(jnp.where(first, zero, flat(rf[:, n, 0, :, 128:256])))
             acc = jnp.dot(jnp.concatenate(slabs, axis=1), w_in[...], preferred_element_type=F32)
             here = d0[2 * sx + a, 1 + 2 * s4 + b] * flat(rf[:, a, b]).astype(F32)
-            loc[a, b] = acc * (1.0 / 72.0) + here
-
-    def whole_image():
-        for a, b in units:
-            full = loc[a, b]
-            if a == 1:
-                full += flat(rco[:, b]).astype(F32)
-            elif b == 1:
-                far = flat(rce[...]).astype(F32)
-                full += jnp.concatenate([jnp.zeros((512, 128), F32), far], axis=1)
-            ri[a, b] = full.astype(BF16)
-
-    def rs_copy(n, k):
-        dz, dx, dy = k % 4, (k // 4) % 4, k // 16
-        m, h, q = ys[dy] * 2 + xhs[dx], xls[dx], zs[dz]
+            ri[a, b] = (acc * (1.0 / 72.0) + here).astype(BF16)
+
+    def nt(left, right):
+        left, right = (jnp.concatenate(parts, axis=1) for parts in (left, right))
+        return lax.dot_general(left, right, NT, preferred_element_type=F32)
+
+    lanes_z = pl.ds(pl.multiple_of(128 * z, 128), 128)
+
+    def margin_y_copy(dy):
+        return remote(half.at[0, ys[dy]], ysum.at[dy], y_s.at[0], y_r.at[0], (sx, ys[dy] * 4 + s4))
+
+    def margin_y_sum():
+        total = half[0, yy].astype(F32)
+        for dy in (1, 2, 3):
+            total += ysum[dy].astype(F32)
+        plane_part[...] = total.astype(BF16)
+
+    def margin_plane_copy(k):
+        dz, dx = k % 4, k // 4
+        lanes = pl.ds(pl.multiple_of(128 * zs[dz], 128), 128)
         return remote(
-            half.at[n, m, h, :, pl.ds(pl.multiple_of(128 * q, 128), 128)],
-            rs.at[n, k], rs_s.at[n], rs_r.at[n], (h * 4 + q, m * 2 + c),
+            plane_part.at[xhs[dx], xls[dx], :, lanes], rs.at[0, k], rs_s.at[0], rs_r.at[0],
+            (xls[dx] * 4 + zs[dz], yy * 4 + xhs[dx] * 2 + c),
         )
 
-    def scatter(n):
-        core_copy(n).wait_recv()
-        half[n] = (gm[:, c] + other[n].astype(F32)).astype(BF16)
-
-        for k in range(1, 64):
-            rs_copy(n, k).start()
-
-        rs[n, 0] = half[n, 2 * yy + xh, xl, :, pl.ds(pl.multiple_of(128 * z, 128), 128)]
-
-    def collect(n):
-        bulk(rs.at[n, 1:64], rs_r.at[n]).wait_recv()
-        ob[sx, n] = jnp.sum(rs[n].astype(F32), axis=0) * ((1.0 - 0.5 * n) / 131072.0)
+    def projected_copies(r, own):
+        for k in range(1 if own else 0, 16):
+            dz, dx = k % 4, k // 4
+            lanes = pl.ds(pl.multiple_of(128 * zs[dz], 128), 128)
+            remote(
+                half.at[1, r, xhs[dx], xls[dx], :, lanes],
+                rs.at[1, 16 * yy + 4 * x + z], rs_s.at[1], rs_r.at[1],
+                (xls[dx] * 4 + zs[dz], r * 4 + xhs[dx] * 2 + c),
+            ).start()
 
     bulk(t.at[1:GROUP], f_r.at[0]).wait_recv()
-    field_rows = jnp.concatenate([flat(rf[:, a, b]) for a, b in units], axis=1)
-    gram(0, field_rows, field_rows)
+    field_rows = [flat(rf[:, a, b]) for a, b in units]
+    for r in range(4):
+        give(0, r, nt([v[128 * r : 128 * r + 128] for v in field_rows], field_rows))
     local_image()
-    scatter(0)
-
+    for r in range(4):
+        take(0, r)
+    for dy in (1, 2, 3):
+        margin_y_copy(dy).start()
+    for r in range(4):
+        gm[1, r] = nt(
+            [v[128 * r : 128 * r + 128] for v in field_rows], [ri[a, b] for a, b in units]
+        ).reshape(2, 2, 2, 16, 512)
     bulk(t.at[1:GROUP, 0], i_r.at[0]).wait_recv()
-    bulk(rs.at[0, 1:GROUP], i_r.at[1]).wait_recv()
-    whole_image()
-    field_rows = [flat(rf[:, a, b]) for a, b in units]
-    image_rows = [ri[a, b] for a, b in units]
-    gram(
-        1,
-        jnp.concatenate(field_rows + image_rows, axis=1),
-        jnp.concatenate(image_rows + field_rows, axis=1),
-    )
-    scatter(1)
-    collect(0)
-    collect(1)
+    bulk(rs.at[1, 0 : GROUP - 1], i_r.at[1]).wait_recv()
+    order = [rem(yy + 1 + i, 4) for i in range(4)]
+    field = [rf[:, 1, 0], rf[:, 1, 1], rf[:, 0, 1, :, 128:256]]
+    across = [rco[:, 0], rco[:, 1], rce[...]]
+    right = [flat(v) for v in across + field]
+    for r in order:
+        eight = pl.ds(8 * r, 8)
+        left = [rf[eight, 1, 0], rf[eight, 1, 1], rf[eight, 0, 1, :, 128:256]]
+        left += [rco[eight, 0], rco[eight, 1], rce[eight]]
+        give(1, r, nt([flat(v) for v in left], right) + gm[1, r].reshape(128, 512))
+    for r in order:
+        take(1, r)
+        projected_copies(r, r is order[3])
+    rs[1, 16 * yy + 4 * x + z] = half[1, yy, xh, xl, :, lanes_z]
+
+    bulk(ysum.at[1:4], y_r.at[0]).wait_recv()
+    margin_y_sum()
+    for k in range(1, 16):
+        margin_plane_copy(k).start()
+    rs[0, 0] = plane_part[xh, xl, :, lanes_z]
+
+    bulk(rs.at[0, 1:16], rs_r.at[0]).wait_recv()
+    ob[sx, 0] = jnp.sum(rs[0, 0:16].astype(F32), axis=0) * (1.0 / 131072.0)
+    bulk(rs.at[1, 0:63], rs_r.at[1]).wait_recv()
+    ob[sx, 1] = jnp.sum(rs[1].astype(F32), axis=0) * (1.0 / 131072.0)
 
     for k in range(1, 8):
         far = rem(sx + k, 8)
@@ -414,7 +438,8 @@
         bulk(t.at[1:GROUP], sem.at[0]).wait_send()
     bulk(t.at[1:GROUP, 0], i_s.at[0]).wait_send()
     bulk(rs.at[0, 1:GROUP], i_s.at[1]).wait_send()
-    bulk(rs.at[0, 1:GROUP], pin_s.at[0]).wait_send()
+    for stage, n in enumerate((3, 12, 16)):
+        bulk(rs.at[0, 0:n], pin_s.at[stage]).wait_send()
 
     def sent(side):
         bulk(u0.at[1:17, 2], hal_s.at[side]).wait_send()
@@ -429,9 +454,12 @@
     def _():
         sent(1)
 
-    for n in range(2):
-        core_copy(n).wait_send()
-        bulk(rs.at[n, 1:64], rs_s.at[n]).wait_send()
+    for r in range(4):
+        core_copy(0, r).wait_send()
+        core_copy(1, r).wait_send()
+    bulk(ysum.at[1:4], y_s.at[0]).wait_send()
+    bulk(rs.at[0, 1:16], rs_s.at[0]).wait_send()
+    bulk(rs.at[1, 0:63], rs_s.at[1]).wait_send()
     bulk(ob.at[0:7], ag_s.at[0]).wait_send()
     bulk(ob.at[0:7], ag_r.at[0]).wait_recv()
     for s in range(8):
@@ -465,19 +493,20 @@
             block,
             pltpu.VMEM((GROUP, 2, 16, 256), BF16),
             pltpu.VMEM((GROUP, 16, 128), BF16),
-            pltpu.VMEM((2, 2, 512, 256), F32),
             pltpu.VMEM((2, 2, 512, 256), BF16),
-            pltpu.VMEM((8, 2, 2, 16, 512), F32),
-            pltpu.VMEM((2, 8, 2, 2, 16, 512), BF16),
-            pltpu.VMEM((2, 8, 2, 16, 512), BF16),
-            pltpu.VMEM((2, 8, 2, 16, 512), BF16),
+            pltpu.VMEM((2, 4, 2, 2, 2, 16, 512), F32),
+            pltpu.VMEM((2, 4, 2, 2, 2, 16, 512), BF16),
+            pltpu.VMEM((2, 4, 2, 2, 16, 512), BF16),
+            pltpu.VMEM((2, 4, 2, 2, 16, 512), BF16),
+            pltpu.VMEM((4, 2, 2, 16, 512), BF16),
+            pltpu.VMEM((2, 2, 16, 512), BF16),
             pltpu.VMEM((2, 64, 16, 128), BF16),
             pltpu.VMEM((8, 2, 16, 128), F32),
-            dma((3,)), dma((1,)), dma((32,)), dma((1,)), dma((1,)),
+            dma((3,)), dma((1,)), dma((32,)), dma((3,)), dma((3,)),
             dma((2,)), dma((2,)), dma((2,)), dma((2,)),
             dma((2,)), dma((2,)),
             dma((1,)), dma((1,)), dma((2,)), dma((2,)),
-            dma((2,)), dma((2,)), dma((2,)), dma((2,)),
+            dma((2, 4)), dma((2, 4)), dma((1,)), dma((1,)), dma((2,)), dma((2,)),
             dma((1,)), dma((1,)),
             pltpu.SemaphoreType.REGULAR, pltpu.SemaphoreType.REGULAR,
         ],

time: 74.8 us -> 69.5 us (0.929)
  Pallas kernels: 70.5 us -> 64.7 us
    pallas_call x1, Pallas kernels: 70.5 us -> 64.7 us  [on_device(): pl.pallas_call(kernel, out_shape=[jax.ShapeDtypeStruct((32, 512), F32)] *...]
where the time goes in v4:
time: 69.5 us; the launch traced here: 68.8 us
  Pallas kernels  64.7 us (93%)
  local copies, waits for them, and re-layouts  2.14 us (3%)
  between operations  1.94 us (3%)
    pallas_call x1, Pallas kernels, on_device(): pl.pallas_call(kernel, out_shape=[jax.ShapeDtypeStruct((32, 512), F32)] *...  64.7 us
    unnamed x4, local copies, waits for them, and re-layouts  2.14 us

profile of v4, /device:TPU:1, one launch (start us, length us, event | category | flops | bytes accessed | tf_op | source)
XLA Modules:
  0.0 68.8 jit_solution(4986851731949654113)
XLA Ops:
  1.9 64.7 %shard_map.68 = (f32[32,512]{1,0:T(8,128)}, f32[32,512]{1,0:T(8,128)}) custom-call(bf16[2,8,64,512]{3,2,1,0:T(8,128)(2,1)} %wave_hbm.1, f32[2,8,64]{2,1,0:T(8,128)} %pot_hbm.1, f32[1]{0:T(128)S(6)} %copy.9.low, f32[1]{0:T(128)S(6)} %copy.10.high, bf16[768,256]{1,0:T(8,128)(2,1)} %constant.2.clone.w_hbm), custom_call_target="tpu_custom_call" | custom-call | tf_op jit(solution)/shard_map/pallas_call | solution.py:479
  66.6 0.0 copy-start
  66.6 1.5 %copy.11 = f32[32,512]{1,0:T(8,128)} copy(f32[32,512]{1,0:T(8,128)} %get-tuple-element.4) | data formatting | bytes 131072
  68.1 0.0 copy-done
  68.1 0.6 copy.12
Async XLA Ops:
  66.6 1.5 %copy-start = (f32[32,512]{1,0:T(8,128)S(1)}, f32[32,512]{1,0:T(8,128)}, u32[]{:S(2)}) copy-start(f32[32,512]{1,0:T(8,128)} %get-tuple-element.5) | copy-start | bytes 196612

commit v5 on v4

--- a/solution.py
+++ b/solution.py
@@ -37,8 +37,8 @@
 
 
 def kernel(
-    wave_hbm, pot_hbm, low, high, w_hbm, margin, projected,
-    wave, pot, w_in, t, u0, u1, u2, u3, u4, co, ce, d0, rf, rco, rce, ri, gm, part, other, half, ysum, plane_part, rs, ob,
+    wave_hbm, pot_hbm, low, high, w_hbm, summed,
+    wave, pot, w_in, t, u0, u1, u2, u3, u4, face, d0, rf, faces, ri, gm, part, other, half, ysum, plane_part, rs, ob,
     load, in_s, in_r, pin_s, pin_r, hal_s, hal_r, phal_s, phal_r, edge_s, edge_r,
     f_s, f_r, i_s, i_r, core_s, core_r, y_s, y_r, rs_s, rs_r, ag_s, ag_r, plane, chip,
 ):
@@ -233,6 +233,7 @@
             out[:, 10] = jnp.zeros((18, 16, 256), BF16)
 
     apply_step(u0, None, u1, 3, 9)
+    apply_step(u1, u0, u2, 4, 8)
 
     def halo_wait(side):
         bulk(u0.at[1:17, 2], hal_r.at[side]).wait_recv()
@@ -249,11 +250,24 @@
     apply_step(u0, None, u1, 1, 3)
     apply_step(u0, None, u1, 9, 11)
     outside_zero(u1)
-    apply_step(u1, u0, u2, 1, 11)
+    apply_step(u1, u0, u2, 1, 4)
+    apply_step(u1, u0, u2, 8, 11)
     outside_zero(u2)
     apply_step(u2, u1, u3, 1, 11)
     outside_zero(u3)
-    apply_step(u3, u2, u4, 2, 10)
+    def send_out(ks):
+        for k in ks:
+            px, p4 = peer(k)
+            remote(
+                u4.at[pl.ds(1 + 2 * px, 2), pl.ds(2 + 2 * p4, 2)],
+                rf.at[j], f_s.at[0], f_r.at[0], (px, yy * 4 + p4),
+            ).start()
+
+    far_order = (*OTHER, *PLANE, *FIRST)
+    for h, parity in ((1 - xl, 1), (xl, 0)):
+        for i in range(2):
+            apply_chunk(u3, u2, u4, 8 * h + 4 * i, 2, 10)
+        send_out([k for k in far_order if (k // 4) % 2 == parity])
 
     def layer(side):
         far = rem(yy + 3 + 2 * side, 4)
@@ -272,15 +286,6 @@
     def _():
         layer(1).start()
 
-    def send_out(src, dst, ss, rr, first):
-        for k in (*OTHER, *PLANE, *FIRST):
-            px, p4 = peer(k)
-            remote(
-                src.at[pl.ds(first + 2 * px, 2), pl.ds(2 * first + 2 * p4, 2)],
-                dst.at[j], ss.at[0], rr.at[0], (px, yy * 4 + p4),
-            ).start()
-
-    send_out(u4, rf, f_s, f_r, 1)
     rf[j] = u4[xs, bs]
 
     @pl.when(yy < 3)
@@ -311,18 +316,18 @@
         join = lambda parts: jnp.concatenate(parts, axis=0)
         lhs = jnp.concatenate([join(own), join(slab_p), join(slab_q)], axis=1)
         acc = jnp.dot(lhs, w_in[256:768], preferred_element_type=F32) * (1.0 / 72.0)
-        co[pl.ds(4 * i, 4)] = acc.astype(BF16).reshape(4, 8, 16, 256)
+        odd = acc.astype(BF16).reshape(4, 4, 2, 16, 256)
+        for n in range(4):
+            face[pl.ds(4 * i, 4), :, n] = odd[:, :, n // 2, :, 128 * (n % 2) : 128 * (n % 2) + 128]
         lhs = jnp.concatenate([join(even_p), join(even_q)], axis=1)
         acc = jnp.dot(lhs, w_in[512:768, 128:256], preferred_element_type=F32) * (1.0 / 72.0)
-        ce[pl.ds(4 * i, 4)] = acc.astype(BF16).reshape(4, 4, 16, 128)
+        face[pl.ds(4 * i, 4), :, 4] = acc.astype(BF16).reshape(4, 4, 16, 128)
 
     for k in (*OTHER, *PLANE, *FIRST):
         px, p4 = peer(k)
         dev = (px, yy * 4 + p4)
-        remote(co.at[px, pl.ds(2 * p4, 2)], rco.at[j], i_s.at[0], i_r.at[0], dev).start()
-        remote(ce.at[px, p4], rce.at[j], i_s.at[1], i_r.at[1], dev).start()
-    rco[j] = co[sx, pl.ds(2 * s4, 2)]
-    rce[j] = ce[sx, s4]
+        remote(face.at[px, p4], faces.at[j], i_s.at[0], i_r.at[0], dev).start()
+    faces[j] = face[sx, s4]
 
     units = [(a, b) for a in range(2) for b in range(2)]
 
@@ -403,17 +408,19 @@
         gm[1, r] = nt(
             [v[128 * r : 128 * r + 128] for v in field_rows], [ri[a, b] for a, b in units]
         ).reshape(2, 2, 2, 16, 512)
-    bulk(t.at[1:GROUP, 0], i_r.at[0]).wait_recv()
-    bulk(rs.at[1, 0 : GROUP - 1], i_r.at[1]).wait_recv()
+    bulk(faces.at[1:GROUP], i_r.at[0]).wait_recv()
     order = [rem(yy + 1 + i, 4) for i in range(4)]
-    field = [rf[:, 1, 0], rf[:, 1, 1], rf[:, 0, 1, :, 128:256]]
-    across = [rco[:, 0], rco[:, 1], rce[...]]
-    right = [flat(v) for v in across + field]
+    def field(js):
+        return [flat(v) for v in (rf[js, 1, 0], rf[js, 1, 1], rf[js, 0, 1, :, 128:256])]
+
+    def across(js):
+        return [flat(faces[js, n]) for n in range(5)]
+
+    every = slice(None)
+    right = across(every) + field(every)
     for r in order:
         eight = pl.ds(8 * r, 8)
-        left = [rf[eight, 1, 0], rf[eight, 1, 1], rf[eight, 0, 1, :, 128:256]]
-        left += [rco[eight, 0], rco[eight, 1], rce[eight]]
-        give(1, r, nt([flat(v) for v in left], right) + gm[1, r].reshape(128, 512))
+        give(1, r, nt(field(eight) + across(eight), right) + gm[1, r].reshape(128, 512))
     for r in order:
         take(1, r)
         projected_copies(r, r is order[3])
@@ -426,9 +433,9 @@
     rs[0, 0] = plane_part[xh, xl, :, lanes_z]
 
     bulk(rs.at[0, 1:16], rs_r.at[0]).wait_recv()
-    ob[sx, 0] = jnp.sum(rs[0, 0:16].astype(F32), axis=0) * (1.0 / 131072.0)
+    ob[sx, 0] = jnp.sum(rs[0, 0:16].astype(F32), axis=0)
     bulk(rs.at[1, 0:63], rs_r.at[1]).wait_recv()
-    ob[sx, 1] = jnp.sum(rs[1].astype(F32), axis=0) * (1.0 / 131072.0)
+    ob[sx, 1] = jnp.sum(rs[1].astype(F32), axis=0)
 
     for k in range(1, 8):
         far = rem(sx + k, 8)
@@ -436,8 +443,7 @@
 
     for sem in (in_s, f_s):
         bulk(t.at[1:GROUP], sem.at[0]).wait_send()
-    bulk(t.at[1:GROUP, 0], i_s.at[0]).wait_send()
-    bulk(rs.at[0, 1:GROUP], i_s.at[1]).wait_send()
+    bulk(faces.at[1:GROUP], i_s.at[0]).wait_send()
     for stage, n in enumerate((3, 12, 16)):
         bulk(rs.at[0, 0:n], pin_s.at[stage]).wait_send()
 
@@ -464,8 +470,8 @@
     bulk(ob.at[0:7], ag_r.at[0]).wait_recv()
     for s in range(8):
         rows, lanes = pl.ds(16 * (s // 4), 16), pl.ds(128 * (s % 4), 128)
-        margin[rows, lanes] = ob[s, 0]
-        projected[rows, lanes] = ob[s, 1]
+        summed[0, rows, lanes] = ob[s, 0]
+        summed[1, rows, lanes] = ob[s, 1]
 
 
 def on_device(wave, potential, lower_cut, upper_edge):
@@ -476,23 +482,21 @@
     hbm = pl.BlockSpec(memory_space=pl.ANY)
     smem = pl.BlockSpec(memory_space=pltpu.SMEM)
     weights = jnp.asarray(stencil_matrix(), BF16)
-    return pl.pallas_call(
+    summed = pl.pallas_call(
         kernel,
-        out_shape=[jax.ShapeDtypeStruct((32, 512), F32)] * 2,
+        out_shape=jax.ShapeDtypeStruct((2, 32, 512), F32),
         in_specs=[hbm, hbm, smem, smem, hbm],
-        out_specs=[vmem, vmem],
+        out_specs=vmem,
         scratch_shapes=[
             pltpu.VMEM(wave.shape, BF16),
             pltpu.VMEM(potential.shape, F32),
             pltpu.VMEM(weights.shape, BF16),
             block,
             field, field, field, field, field,
-            pltpu.VMEM((8, 8, 16, 256), BF16),
-            pltpu.VMEM((8, 4, 16, 128), BF16),
+            pltpu.VMEM((8, 4, 5, 16, 128), BF16),
             pltpu.VMEM((16, 10, 1, 256), F32),
             block,
-            pltpu.VMEM((GROUP, 2, 16, 256), BF16),
-            pltpu.VMEM((GROUP, 16, 128), BF16),
+            pltpu.VMEM((GROUP, 5, 16, 128), BF16),
             pltpu.VMEM((2, 2, 512, 256), BF16),
             pltpu.VMEM((2, 4, 2, 2, 2, 16, 512), F32),
             pltpu.VMEM((2, 4, 2, 2, 2, 16, 512), BF16),
@@ -505,7 +509,7 @@
             dma((3,)), dma((1,)), dma((32,)), dma((3,)), dma((3,)),
             dma((2,)), dma((2,)), dma((2,)), dma((2,)),
             dma((2,)), dma((2,)),
-            dma((1,)), dma((1,)), dma((2,)), dma((2,)),
+            dma((1,)), dma((1,)), dma((1,)), dma((1,)),
             dma((2, 4)), dma((2, 4)), dma((1,)), dma((1,)), dma((2,)), dma((2,)),
             dma((1,)), dma((1,)),
             pltpu.SemaphoreType.REGULAR, pltpu.SemaphoreType.REGULAR,
@@ -514,6 +518,7 @@
             collective_id=0, has_side_effects=True, vmem_limit_bytes=127 << 19
         ),
     )(wave, potential, lower_cut, upper_edge, weights)
+    return summed[0] * (1.0 / 131072.0), summed[1] * (1.0 / 131072.0)
 
 
 def solution(mesh):

time: 69.5 us -> 68 us (0.978)
  local copies, waits for them, and re-layouts: 2.14 us -> 0 us
  other arithmetic: 0 us -> 1.53 us
  Pallas kernels: 64.7 us -> 64 us
    unnamed x4 -> x0, local copies, waits for them, and re-layouts: 2.14 us -> none
    mul x0 -> x1, other arithmetic: none -> 1.53 us  [on_device(): return (summed[0] * (1.0 / 131072.0), summed[1] * (1.0 / 131072.0))]
    pallas_call x1, Pallas kernels: 64.7 us -> 64 us  [on_device(): pl.pallas_call(kernel, out_shape=jax.ShapeDtypeStruct((2, 32, 512), F32),...]
where the time goes in v5:
time: 68 us; the launch traced here: 67.4 us
  Pallas kernels  64 us (94%)
  between operations  1.93 us (3%)
  other arithmetic  1.53 us (2%)
    pallas_call x1, Pallas kernels, on_device(): pl.pallas_call(kernel, out_shape=jax.ShapeDtypeStruct((2, 32, 512), F32),...  64 us
    mul x1, other arithmetic, on_device(): return (summed[0] * (1.0 / 131072.0), summed[1] * (1.0 / 131072.0))  1.53 us

profile of v5, /device:TPU:1, one launch (start us, length us, event | category | flops | bytes accessed | tf_op | source)
XLA Modules:
  0.0 67.4 jit_solution(7056758259250398569)
XLA Ops:
  1.9 64.0 %shard_map.68 = f32[2,32,512]{2,1,0:T(8,128)} custom-call(bf16[2,8,64,512]{3,2,1,0:T(8,128)(2,1)} %wave_hbm.1, f32[2,8,64]{2,1,0:T(8,128)} %pot_hbm.1, f32[1]{0:T(128)S(6)} %copy.7.low, f32[1]{0:T(128)S(6)} %copy.8.high, bf16[768,256]{1,0:T(8,128)(2,1)} %constant.4.clone.w_hbm), custom_call_target="tpu_custom_call" | custom-call | tf_op jit(solution)/shard_map/pallas_call | solution.py:485
  65.9 1.5 %multiply_bitcast_fusion = (f32[32,512]{1,0:T(8,128)}, f32[32,512]{1,0:T(8,128)}) fusion(f32[2,32,512]{2,1,0:T(8,128)} %shard_map.68), kind=kLoop, calls=%fused_computation | loop fusion | flops 32768 | bytes 262144 | tf_op jit(solution)/shard_map/mul | solution.py:521

commit v6 on v5

--- a/solution.py
+++ b/solution.py
@@ -386,7 +386,7 @@
         )
 
     def projected_copies(r, own):
-        for k in range(1 if own else 0, 16):
+        for k in (*PLANE, *FIRST) if own else (*PLANE, *FIRST, 0):
             dz, dx = k % 4, k // 4
             lanes = pl.ds(pl.multiple_of(128 * zs[dz], 128), 128)
             remote(
@@ -409,7 +409,7 @@
             [v[128 * r : 128 * r + 128] for v in field_rows], [ri[a, b] for a, b in units]
         ).reshape(2, 2, 2, 16, 512)
     bulk(faces.at[1:GROUP], i_r.at[0]).wait_recv()
-    order = [rem(yy + 1 + i, 4) for i in range(4)]
+    order = [rem(yy + i, 4) for i in (2, 1, 3, 0)]
     def field(js):
         return [flat(v) for v in (rf[js, 1, 0], rf[js, 1, 1], rf[js, 0, 1, :, 128:256])]
 

time: 68 us -> 67.9 us (level)
  no operation moved by 1% of the time
where the time goes in v6:
time: 67.9 us; the launch traced here: 67.1 us
  Pallas kernels  63.6 us (94%)
  between operations  1.93 us (3%)
  other arithmetic  1.53 us (2%)
    pallas_call x1, Pallas kernels, on_device(): pl.pallas_call(kernel, out_shape=jax.ShapeDtypeStruct((2, 32, 512), F32),...  63.6 us
    mul x1, other arithmetic, on_device(): return (summed[0] * (1.0 / 131072.0), summed[1] * (1.0 / 131072.0))  1.53 us

profile of v6, /device:TPU:1, one launch (start us, length us, event | category | flops | bytes accessed | tf_op | source)
XLA Modules:
  0.0 67.1 jit_solution(12538027544903756914)
XLA Ops:
  1.9 63.6 %shard_map.68 = f32[2,32,512]{2,1,0:T(8,128)} custom-call(bf16[2,8,64,512]{3,2,1,0:T(8,128)(2,1)} %wave_hbm.1, f32[2,8,64]{2,1,0:T(8,128)} %pot_hbm.1, f32[1]{0:T(128)S(6)} %copy.7.low, f32[1]{0:T(128)S(6)} %copy.8.high, bf16[768,256]{1,0:T(8,128)(2,1)} %constant.4.clone.w_hbm), custom_call_target="tpu_custom_call" | custom-call | tf_op jit(solution)/shard_map/pallas_call | solution.py:485
  65.5 1.5 %multiply_bitcast_fusion = (f32[32,512]{1,0:T(8,128)}, f32[32,512]{1,0:T(8,128)}) fusion(f32[2,32,512]{2,1,0:T(8,128)} %shard_map.68), kind=kLoop, calls=%fused_computation | loop fusion | flops 32768 | bytes 262144 | tf_op jit(solution)/shard_map/mul | solution.py:521

commit v7 on v6

--- a/solution.py
+++ b/solution.py
@@ -113,10 +113,13 @@
     bs = pl.ds(2 + 2 * s4, 2)
     own_pot = d0.at[pl.ds(2 * sx, 2), pl.ds(1 + 2 * s4, 2)]
 
+    has_edge = 1 - (xh + c - 2 * xh * c)
+    in_slot = has_edge * (2 * sx + c) + (1 - has_edge) * 16
+
     def in_copy(k):
         px, p4 = peer(k)
         return remote(
-            t.at[px * 4 + p4], u0.at[xs, bs], in_s.at[0], in_r.at[j], (px, yy * 4 + p4)
+            t.at[px * 4 + p4], u0.at[xs, bs], in_s.at[0], in_r.at[in_slot], (px, yy * 4 + p4)
         )
 
     def send_in(ks):
@@ -174,18 +177,22 @@
     def _():
         pot_edge(1).start()
 
-    def arrived(i):
-        @pl.when(j != i)
-        def _():
-            bulk(u0.at[xs, bs], in_r.at[i]).wait_recv()
-
     for s in range(8):
         for quarter in (0, 3):
-            arrived(4 * s + quarter)
+
+            @pl.when(j != 4 * s + quarter)
+            def _():
+                bulk(u0.at[xs, bs], in_r.at[2 * s + quarter // 3]).wait_recv()
+
             send_on(s, quarter)
-    for s in range(8):
-        for quarter in (1, 2):
-            arrived(4 * s + quarter)
+
+    @pl.when(has_edge == 1)
+    def _():
+        bulk(t.at[0:16], in_r.at[16]).wait_recv()
+
+    @pl.when(has_edge == 0)
+    def _():
+        bulk(t.at[0:15], in_r.at[16]).wait_recv()
 
     loads[2].wait()
     centre = 0.5 * (high[0] + low[0])
@@ -336,7 +343,7 @@
 
     def core_copy(n, r):
         return remote(
-            part.at[n, r, :, 1 - c], other.at[n, r], core_s.at[n, r], core_r.at[n, r], sibling
+            part.at[n, r, :, 1 - c], other.at[n, r], core_s.at[n], core_r.at[n, r], sibling
         )
 
     def give(n, r, g):
@@ -460,9 +467,8 @@
     def _():
         sent(1)
 
-    for r in range(4):
-        core_copy(0, r).wait_send()
-        core_copy(1, r).wait_send()
+    for n in range(2):
+        bulk(other.at[n], core_s.at[n]).wait_send()
     bulk(ysum.at[1:4], y_s.at[0]).wait_send()
     bulk(rs.at[0, 1:16], rs_s.at[0]).wait_send()
     bulk(rs.at[1, 0:63], rs_s.at[1]).wait_send()
@@ -506,11 +512,11 @@
             pltpu.VMEM((2, 2, 16, 512), BF16),
             pltpu.VMEM((2, 64, 16, 128), BF16),
             pltpu.VMEM((8, 2, 16, 128), F32),
-            dma((3,)), dma((1,)), dma((32,)), dma((3,)), dma((3,)),
+            dma((3,)), dma((1,)), dma((17,)), dma((3,)), dma((3,)),
             dma((2,)), dma((2,)), dma((2,)), dma((2,)),
             dma((2,)), dma((2,)),
             dma((1,)), dma((1,)), dma((1,)), dma((1,)),
-            dma((2, 4)), dma((2, 4)), dma((1,)), dma((1,)), dma((2,)), dma((2,)),
+            dma((2,)), dma((2, 4)), dma((1,)), dma((1,)), dma((2,)), dma((2,)),
             dma((1,)), dma((1,)),
             pltpu.SemaphoreType.REGULAR, pltpu.SemaphoreType.REGULAR,
         ],

time: 67.9 us -> 67.7 us (level)
  no operation moved by 1% of the time
where the time goes in v7:
time: 67.7 us; the launch traced here: 66.9 us
  Pallas kernels  63.4 us (94%)
  between operations  1.93 us (3%)
  other arithmetic  1.53 us (2%)
    pallas_call x1, Pallas kernels, on_device(): pl.pallas_call(kernel, out_shape=jax.ShapeDtypeStruct((2, 32, 512), F32),...  63.4 us
    mul x1, other arithmetic, on_device(): return (summed[0] * (1.0 / 131072.0), summed[1] * (1.0 / 131072.0))  1.53 us

profile of v7, /device:TPU:1, one launch (start us, length us, event | category | flops | bytes accessed | tf_op | source)
XLA Modules:
  0.0 66.9 jit_solution(14059705398218651882)
XLA Ops:
  1.9 63.4 %shard_map.68 = f32[2,32,512]{2,1,0:T(8,128)} custom-call(bf16[2,8,64,512]{3,2,1,0:T(8,128)(2,1)} %wave_hbm.1, f32[2,8,64]{2,1,0:T(8,128)} %pot_hbm.1, f32[1]{0:T(128)S(6)} %copy.7.low, f32[1]{0:T(128)S(6)} %copy.8.high, bf16[768,256]{1,0:T(8,128)(2,1)} %constant.4.clone.w_hbm), custom_call_target="tpu_custom_call" | custom-call | tf_op jit(solution)/shard_map/pallas_call | solution.py:491
  65.3 1.5 %multiply_bitcast_fusion = (f32[32,512]{1,0:T(8,128)}, f32[32,512]{1,0:T(8,128)}) fusion(f32[2,32,512]{2,1,0:T(8,128)} %shard_map.68), kind=kLoop, calls=%fused_computation | loop fusion | flops 32768 | bytes 262144 | tf_op jit(solution)/shard_map/mul | solution.py:527
